TPU v7x, 512 devices: a whole 4x8x8 slice. The times are simulated.
512 devices in a mesh: group: 32 (over y, x), member: 16 (over z, core).
Axes of the slice: x: 4, y: 8, z: 8, core: 2. Of those that a mesh axis runs over, the one named last changes fastest.
Arguments:
- passages: bfloat16 [524288, 768], P(('group', 'member')), may hold values from -32 to 32
- labels: int32 [524288], P(('group', 'member')), may hold values from 0 to 127
- send_counts: int32 [512, 32], P(('group', 'member')), may hold values from 24 to 40, as said below
- send_offsets: int32 [512, 32], P(('group', 'member')), may hold values from 0 to 1024, as said below
- owner_slot: int32 [128], replicated, may hold values from 0 to 127, as said below
- centroids: bfloat16 [12800, 768], P(('group', 'member')), may hold values from -2 to 2
Outputs:
- new_centroids: float32 [12800, 768], P(('group', 'member'))
Inputs may be any that keep to these rules, and one draw needn't show every extreme that they name: On each device, rows send_offsets[g] to send_offsets[g] + send_counts[g] - 1 hold the passages whose cluster is owned by group g, that is owner_slot[label] // 4 = g. `send_counts`: A device sends at most 40 passages to one group, and its counts sum to 1024; in every draw some group receives 40 from every device. A permutation of the slots; cluster c is owned by group owner_slot[c] // 4.
All inputs are finite; a program needn't handle non-finite values.
Results may differ from a plain program's by a relative error of at most 0.003.
Values may be sent and summed in bfloat16 or wider, within the bound.
No kernel may reach another device: no remote copies, remote signals or barrier semaphores. Data moves between devices by JAX's collectives and lax.ppermute only.
A program may use at most 64 MiB of HBM per device.

v0:
```python
import jax
import jax.numpy as jnp
from jax import lax
from jax.sharding import PartitionSpec as P

K = 100
CL_GRP = 4
ITERS = 2


temper = 16.0


def shards(passages, labels, send_counts, send_offsets, owner_slot, centroids):
    groups = lax.axis_size("group")
    rows_dev, features = passages.shape
    capacity = 5 * rows_dev // (4 * groups)
    clusters = owner_slot.shape[0]
    matches = labels[:, None] == jnp.arange(clusters, dtype=jnp.int32)[None, :]
    slot_of_row = jnp.sum(jnp.where(matches, owner_slot[None, :], 0), axis=1)
    local_slot = slot_of_row % CL_GRP
    slot_index = jnp.arange(capacity, dtype=jnp.int32)[None, :]
    usable = slot_index < send_counts[0][:, None]
    source_rows = jnp.where(
        usable, jnp.minimum(send_offsets[0][:, None] + slot_index, rows_dev - 1), 0
    )
    outgoing = jnp.where(
        usable[:, :, None], jnp.take(passages, source_rows, axis=0), jnp.zeros((), jnp.bfloat16)
    )
    slot_tags = jnp.where(usable, jnp.take(local_slot, source_rows), -1)
    arrived, arrived_tags = (
        lax.all_to_all(outgoing, "group", split_axis=0, concat_axis=0, tiled=True),
        lax.all_to_all(slot_tags, "group", split_axis=0, concat_axis=0, tiled=True),
    )
    arrived = arrived.reshape(groups * capacity, features)
    arrived_tags = arrived_tags.reshape(groups * capacity)
    ownership = (arrived_tags[None, :] == jnp.arange(CL_GRP, dtype=jnp.int32)[:, None]).astype(
        jnp.float32
    )
    slot_rows = centroids.shape[0]
    own_rows = centroids.astype(jnp.float32)
    for sweep in range(ITERS):
        panel_rows = lax.all_gather(own_rows.astype(jnp.bfloat16), "member", axis=0, tiled=True)
        lengths = jnp.sum(jnp.square(panel_rows.astype(jnp.float32)), axis=1)
        product = lax.dot_general(
            panel_rows, arrived, (((1,), (1,)), ((), ())), preferred_element_type=jnp.float32
        )
        logits = ((2.0 * product - lengths[:, None]) / temper).reshape(CL_GRP, K, -1)
        highest = jnp.max(logits, axis=1, keepdims=True)
        exponent = jnp.exp(logits - highest)
        weights = exponent / jnp.sum(exponent, axis=1, keepdims=True) * ownership[:, None, :]
        weights = weights.reshape(CL_GRP * K, -1)
        totals = jnp.sum(weights, axis=1)
        numerator = jnp.dot(
            weights.astype(jnp.bfloat16), arrived, preferred_element_type=jnp.float32
        )
        numerator, totals = (numerator, totals)
        numerator_own = lax.psum_scatter(numerator, "member", scatter_dimension=0, tiled=True)
        totals_all = lax.psum(totals, "member")
        totals_own = lax.dynamic_slice_in_dim(
            totals_all, lax.axis_index("member") * slot_rows, slot_rows, 0
        )
        own_rows = (numerator_own + own_rows) / (totals_own[:, None] + 1.0)
    return own_rows


def solution(mesh):
    return jax.shard_map(
        shards,
        mesh=mesh,
        in_specs=(
            P(("group", "member"), None),
            P(("group", "member")),
            P(("group", "member"), None),
            P(("group", "member"), None),
            P(),
            P(("group", "member"), None),
        ),
        out_specs=P(("group", "member"), None),
        check_vma=False,
    )
```

profile of v0, /device:TPU:1, one launch (start us, length us, event | category | flops | bytes accessed | tf_op | source)
XLA Modules:
  0.0 294.4 jit_solution(585029949278544431)
XLA Ops:
  2.1 5.0 %gather_fusion.1 = s32[1280]{0:T(1024)S(1)} fusion(s32[1024]{0:T(1024)S(1)} %add_select_fusion, s32[2048]{0:T(1024)S(1)} %pad_clamp_fusion), kind=kCustom, calls=%fused_computation.1 | custom fusion | bytes 15360 | tf_op jit(solution)/shard_map/jit(_take)/gather | solution.py:30
  7.9 10.6 %all-to-all-start.1 = ((s32[32,1,40]{2,1,0:T(1,128)}), s32[32,1,40]{2,1,0:T(1,128)}, u32[]{:S(2)}, u32[]{:S(2)}) async-start(s32[32,1,40]{2,1,0:T(1,128)} %compare_select_fusion.3), calls=%async_computation.1 | async-start | bytes 32768 | tf_op jit(solution)/shard_map/all_to_all | solution.py:33
  18.7 4.2 %gather_fusion = bf16[1280,768]{1,0:T(8,128)(2,1)S(1)} fusion(bf16[1024,768]{1,0:T(8,128)(2,1)S(1)} %copy-done, s32[2048]{0:T(1024)S(1)} %pad_clamp_fusion), kind=kCustom, calls=%fused_computation | custom fusion | bytes 3937280 | tf_op jit(solution)/shard_map/jit(_take)/gather | solution.py:28
  24.4 2.6 all-to-all-done.1
  27.0 6.8 %all-to-all-start = ((bf16[32,40,768]{2,1,0:T(8,128)(2,1)}), bf16[32,40,768]{2,1,0:T(8,128)(2,1)}, u32[]{:S(2)}, u32[]{:S(2)}) async-start(bf16[32,40,768]{2,1,0:T(8,128)(2,1)} %select_select_fusion), calls=%async_computation | async-start | bytes 3932160 | tf_op jit(solution)/shard_map/all_to_all | solution.py:32
  33.9 26.7 %all-gather = bf16[16,25,768]{2,1,0:T(8,128)(2,1)S(1)} all-gather(bf16[1,25,768]{2,1,0:T(8,128)(2,1)S(1)} %bitcast.25), channel_id=1, replica_groups=mesh['group'=32,'member'=16] {'member'}, dimensions={0}, use_global_device_ids=true | all-gather | bytes 652800 | tf_op jit(solution)/shard_map/all_gather | solution.py:43
  66.4 3.1 %mul.31 = f32[400,1280]{1,0:T(8,128)} reshape(f32[4,100,1280]{2,1,0:T(8,128)} %mul.30) | data formatting | bytes 4096000 | tf_op jit(solution)/shard_map/mul | solution.py:51
  69.5 9.8 %all-to-all-done = bf16[32,40,768]{2,1,0:T(8,128)(2,1)} async-done(((bf16[32,40,768]{2,1,0:T(8,128)(2,1)}), bf16[32,40,768]{2,1,0:T(8,128)(2,1)}, u32[]{:S(2)}, u32[]{:S(2)}) %all-to-all-start) | async-done | bytes 1966112 | tf_op jit(solution)/shard_map/all_to_all | solution.py:32
  79.3 3.9 %fusion.8 = f32[400,1280]{1,0:T(8,128)} fusion(bf16[1280,768]{1,0:T(8,128)(2,1)} %bitcast.3, bf16[400,768]{1,0:T(8,128)(2,1)S(1)} %reshape.328, f32[400]{0:T(512)S(1)} %multiply_reduce_fusion.1), kind=kOutput, calls=%fused_computation.10 | convolution fusion | flops 787968000 | bytes 4630080 | tf_op jit(solution)/shard_map/dot_general | solution.py:45
  83.2 3.1 %reshape.306 = f32[4,100,1280]{2,1,0:T(8,128)} reshape(f32[400,1280]{1,0:T(8,128)} %fusion.8) | data formatting | bytes 4096000 | tf_op jit(solution)/shard_map/reshape | solution.py:48
  86.3 1.7 reduce_max.18
  88.0 3.3 %fusion.3 = f32[4,100,1280]{2,1,0:T(8,128)} fusion(f32[4,100,1280]{2,1,0:T(8,128)} %reshape.306, f32[4,1280]{1,0:T(4,128)S(1)} %reduce_max.18), kind=kOutput, calls=%fused_computation.3 | output fusion | flops 517219 | bytes 4116480 | tf_op jit(solution)/shard_map/div | solution.py:51
  91.3 3.1 %div.49 = f32[400,1280]{1,0:T(8,128)} reshape(f32[4,100,1280]{2,1,0:T(8,128)} %fusion.3) | data formatting | bytes 4096000 | tf_op jit(solution)/shard_map/div | solution.py:51
  95.8 3.2 %sub.46 = f32[400,1280]{1,0:T(8,128)} reshape(f32[4,100,1280]{2,1,0:T(8,128)} %sub.45) | data formatting | bytes 4096000 | tf_op jit(solution)/shard_map/sub | solution.py:50
  99.0 4.1 %fusion.27 = (f32[400]{0:T(512)S(1)}, bf16[400,1280]{1,0:T(8,128)(2,1)S(1)}) fusion(f32[400,1280]{1,0:T(8,128)} %mul.31, f32[400,1280]{1,0:T(8,128)} %div.49, f32[400,1280]{1,0:T(8,128)} %fusion.8, f32[400,1280]{1,0:T(8,128)} %sub.46), kind=kLoop, calls=%fused_computation.56 | loop fusion | flops 2559600 | bytes 9217600 | tf_op jit(solution)/shard_map/reduce_sum | solution.py:53
  103.1 2.5 fusion.17
  105.6 37.5 %fusion = f32[32,768]{1,0:T(8,128)S(1)} fusion(f32[400,768]{1,0:T(8,128)S(1)} %fusion.17), kind=kCustom, calls=%all-reduce-scatter | all-reduce-scatter fusion | flops 393217 | bytes 1329152
  144.5 2.6 collective-permute-start.1
  147.0 3.8 %collective-permute-start = (f32[32,768]{1,0:T(8,128)S(1)}, f32[32,768]{1,0:T(8,128)S(1)}, u32[]{:S(2)}, u32[]{:S(2)}) collective-permute-start(f32[32,768]{1,0:T(8,128)S(1)} %fusion), channel_id=1, source_target_pairs={{0,1},{1,2},{2,3},{3,4},{4,5},{5,6},{6,7},{7,8},{8,9},{9,10},{10,1... | collective-permute-start | bytes 294920
  150.8 23.0 %psum.14 = f32[400]{0:T(512)S(1)} all-reduce(f32[400]{0:T(512)S(1)} %get-tuple-element.7), channel_id=1, replica_groups=mesh['group'=32,'member'=16] {'member'}, use_global_device_ids=true, to_apply=%region_6.7 | all-reduce | flops 400 | bytes 3200 | tf_op jit(solution)/shard_map/psum | solution.py:59
  177.3 23.6 %all-gather.1 = bf16[16,25,768]{2,1,0:T(8,128)(2,1)S(1)} all-gather(bf16[1,25,768]{2,1,0:T(8,128)(2,1)S(1)} %convert_bitcast_fusion), channel_id=1, replica_groups=mesh['group'=32,'member'=16] {'member'}, dimensions={0}, use_global_device_ids=true | all-gather | bytes 652800 | tf_op jit(solution)/shard_map/all_gather | solution.py:43
  201.3 3.9 %fusion.5 = f32[400,1280]{1,0:T(8,128)} fusion(bf16[400,768]{1,0:T(8,128)(2,1)S(1)} %reshape.330, bf16[1280,768]{1,0:T(8,128)(2,1)} %bitcast.3, f32[400]{0:T(512)S(1)} %multiply_reduce_fusion), kind=kOutput, calls=%fused_computation.6 | convolution fusion | flops 787968000 | bytes 4630080 | tf_op jit(solution)/shard_map/dot_general | solution.py:45
  205.2 3.1 %reshape.307 = f32[4,100,1280]{2,1,0:T(8,128)} reshape(f32[400,1280]{1,0:T(8,128)} %fusion.5) | data formatting | bytes 4096000 | tf_op jit(solution)/shard_map/reshape | solution.py:48
  210.0 3.3 %fusion.2 = f32[4,100,1280]{2,1,0:T(8,128)} fusion(f32[4,100,1280]{2,1,0:T(8,128)} %reshape.307, f32[4,1280]{1,0:T(4,128)S(1)} %reduce_max.19), kind=kOutput, calls=%fused_computation.2 | output fusion | flops 517219 | bytes 4116480 | tf_op jit(solution)/shard_map/div | solution.py:51
  213.3 3.1 %div.55 = f32[400,1280]{1,0:T(8,128)} reshape(f32[4,100,1280]{2,1,0:T(8,128)} %fusion.2) | data formatting | bytes 4096000 | tf_op jit(solution)/shard_map/div | solution.py:51
  217.8 3.2 %sub.52 = f32[400,1280]{1,0:T(8,128)} reshape(f32[4,100,1280]{2,1,0:T(8,128)} %sub.51) | data formatting | bytes 4096000 | tf_op jit(solution)/shard_map/sub | solution.py:50
  221.0 4.1 %fusion.26 = (f32[400]{0:T(512)S(1)}, bf16[400,1280]{1,0:T(8,128)(2,1)S(1)}) fusion(f32[400,1280]{1,0:T(8,128)} %mul.31, f32[400,1280]{1,0:T(8,128)} %div.55, f32[400,1280]{1,0:T(8,128)} %fusion.5, f32[400,1280]{1,0:T(8,128)} %sub.52), kind=kLoop, calls=%fused_computation.55 | loop fusion | flops 2559600 | bytes 9217600 | tf_op jit(solution)/shard_map/reduce_sum | solution.py:53
  225.1 2.5 fusion.15
  227.6 30.2 %fusion.1 = f32[32,768]{1,0:T(8,128)S(1)} fusion(f32[400,768]{1,0:T(8,128)S(1)} %fusion.15), kind=kCustom, calls=%all-reduce-scatter.1 | all-reduce-scatter fusion | flops 393217 | bytes 1329152
  259.1 4.4 %collective-permute-start.5 = (f32[32,768]{1,0:T(8,128)S(1)}, f32[32,768]{1,0:T(8,128)S(1)}, u32[]{:S(2)}, u32[]{:S(2)}) collective-permute-start(f32[32,768]{1,0:T(8,128)S(1)} %fusion.1), channel_id=1, source_target_pairs={{0,2},{1,3},{2,4},{3,5},{4,6},{5,7},{6,8},{7,9},{8,10},{9,11},{10,... | collective-permute-start | bytes 294920
  263.5 3.8 %collective-permute-start.4 = (f32[32,768]{1,0:T(8,128)S(1)}, f32[32,768]{1,0:T(8,128)S(1)}, u32[]{:S(2)}, u32[]{:S(2)}) collective-permute-start(f32[32,768]{1,0:T(8,128)S(1)} %fusion.1), channel_id=1, source_target_pairs={{0,1},{1,2},{2,3},{3,4},{4,5},{5,6},{6,7},{7,8},{8,9},{9,10},{10,1... | collective-permute-start | bytes 294920
  267.3 23.0 %psum.15 = f32[400]{0:T(512)S(1)} all-reduce(f32[400]{0:T(512)S(1)} %get-tuple-element.5), channel_id=1, replica_groups=mesh['group'=32,'member'=16] {'member'}, use_global_device_ids=true, to_apply=%region_12.13 | all-reduce | flops 400 | bytes 3200 | tf_op jit(solution)/shard_map/psum | solution.py:59
  (50 shorter events, 24.9 us)
Async XLA Ops:
  0.0 18.6 %copy-start = (bf16[1024,768]{1,0:T(8,128)(2,1)S(1)}, bf16[1024,768]{1,0:T(8,128)(2,1)}, u32[]{:S(2)}) copy-start(bf16[1024,768]{1,0:T(8,128)(2,1)} %param.6) | copy-start | bytes 4718596
  2.1 5.1 %copy-start.2 = (s32[1,32]{1,0:T(1,128)S(1)}, s32[1,32]{1,0:T(1,128)}, u32[]{:S(2)}) copy-start(s32[1,32]{1,0:T(1,128)} %param.9) | copy-start | bytes 388
  2.1 5.1 %copy-start.3 = (s32[1,32]{1,0:T(1,128)S(1)}, s32[1,32]{1,0:T(1,128)}, u32[]{:S(2)}) copy-start(s32[1,32]{1,0:T(1,128)} %param.8) | copy-start | bytes 388
  7.9 19.1 %all-to-all-start.1 = ((s32[32,1,40]{2,1,0:T(1,128)}), s32[32,1,40]{2,1,0:T(1,128)}, u32[]{:S(2)}, u32[]{:S(2)}) async-start(s32[32,1,40]{2,1,0:T(1,128)} %compare_select_fusion.3), calls=%async_computation.1 | async-start | bytes 32768 | tf_op jit(solution)/shard_map/all_to_all | solution.py:33
  24.4 9.4 %copy-start.1 = (bf16[25,768]{1,0:T(8,128)(2,1)S(1)}, bf16[25,768]{1,0:T(8,128)(2,1)}, u32[]{:S(2)}) copy-start(bf16[25,768]{1,0:T(8,128)(2,1)} %param.11) | copy-start | bytes 115204
  27.0 52.2 %all-to-all-start = ((bf16[32,40,768]{2,1,0:T(8,128)(2,1)}), bf16[32,40,768]{2,1,0:T(8,128)(2,1)}, u32[]{:S(2)}, u32[]{:S(2)}) async-start(bf16[32,40,768]{2,1,0:T(8,128)(2,1)} %select_select_fusion), calls=%async_computation | async-start | bytes 3932160 | tf_op jit(solution)/shard_map/all_to_all | solution.py:32
  143.2 33.4 %collective-permute-start.2 = (f32[32,768]{1,0:T(8,128)S(1)}, f32[32,768]{1,0:T(8,128)S(1)}, u32[]{:S(2)}, u32[]{:S(2)}) collective-permute-start(f32[32,768]{1,0:T(8,128)S(1)} %fusion), channel_id=1, source_target_pairs={{0,3},{1,4},{2,5},{3,6},{4,7},{5,8},{6,9},{7,10},{8,11},{9,12},{10... | collective-permute-start | bytes 294920
  144.5 32.1 %collective-permute-start.1 = (f32[32,768]{1,0:T(8,128)S(1)}, f32[32,768]{1,0:T(8,128)S(1)}, u32[]{:S(2)}, u32[]{:S(2)}) collective-permute-start(f32[32,768]{1,0:T(8,128)S(1)} %fusion), channel_id=1, source_target_pairs={{0,2},{1,3},{2,4},{3,5},{4,6},{5,7},{6,8},{7,9},{8,10},{9,11},{10,... | collective-permute-start | bytes 294920
  147.0 29.5 %collective-permute-start = (f32[32,768]{1,0:T(8,128)S(1)}, f32[32,768]{1,0:T(8,128)S(1)}, u32[]{:S(2)}, u32[]{:S(2)}) collective-permute-start(f32[32,768]{1,0:T(8,128)S(1)} %fusion), channel_id=1, source_target_pairs={{0,1},{1,2},{2,3},{3,4},{4,5},{5,6},{6,7},{7,8},{8,9},{9,10},{10,1... | collective-permute-start | bytes 294920
  173.8 2.7 collective-permute-start.3
  257.8 35.2 %collective-permute-start.6 = (f32[32,768]{1,0:T(8,128)S(1)}, f32[32,768]{1,0:T(8,128)S(1)}, u32[]{:S(2)}, u32[]{:S(2)}) collective-permute-start(f32[32,768]{1,0:T(8,128)S(1)} %fusion.1), channel_id=1, source_target_pairs={{0,3},{1,4},{2,5},{3,6},{4,7},{5,8},{6,9},{7,10},{8,11},{9,12},{10... | collective-permute-start | bytes 294920
  259.1 33.9 %collective-permute-start.5 = (f32[32,768]{1,0:T(8,128)S(1)}, f32[32,768]{1,0:T(8,128)S(1)}, u32[]{:S(2)}, u32[]{:S(2)}) collective-permute-start(f32[32,768]{1,0:T(8,128)S(1)} %fusion.1), channel_id=1, source_target_pairs={{0,2},{1,3},{2,4},{3,5},{4,6},{5,7},{6,8},{7,9},{8,10},{9,11},{10,... | collective-permute-start | bytes 294920
  263.5 29.5 %collective-permute-start.4 = (f32[32,768]{1,0:T(8,128)S(1)}, f32[32,768]{1,0:T(8,128)S(1)}, u32[]{:S(2)}, u32[]{:S(2)}) collective-permute-start(f32[32,768]{1,0:T(8,128)S(1)} %fusion.1), channel_id=1, source_target_pairs={{0,1},{1,2},{2,3},{3,4},{4,5},{5,6},{6,7},{7,8},{8,9},{9,10},{10,1... | collective-permute-start | bytes 294920
  290.3 2.7 collective-permute-start.7
where the time goes:
time: 298 us; the launch traced here: 294 us
  blocking collectives  164 us (55%)
  local copies, waits for them, and re-layouts  39.3 us (13%)
  starting transfers between devices  37.6 us (13%)
  other arithmetic  25.3 us (8%)
  waiting for transfers between devices  14.6 us (5%)
  matrix products  12.8 us (4%)
    unnamed x2, blocking collectives  67.7 us
    all_gather x2, blocking collectives, shards(): lax.all_gather(own_rows.astype(jnp.bfloat16), 'member', axis=0, tiled=True)  50.3 us
    psum x2, blocking collectives, shards(): totals_all = lax.psum(totals, 'member')  46 us
    unnamed x8, starting transfers between devices  20.1 us
    all_to_all x1, starting transfers between devices, shards(): lax.all_to_all(slot_tags, 'group', split_axis=0, concat_axis=0, tiled=True)  10.6 us
    all_to_all x1, waiting for transfers between devices, shards(): lax.all_to_all(outgoing, 'group', split_axis=0, concat_axis=0, tiled=True)  9.81 us
    sub x4, local copies, waits for them, and re-layouts, shards(): exponent = jnp.exp(logits - highest)  9.33 us
    reduce_sum x2, other arithmetic, shards(): totals = jnp.sum(weights, axis=1)  8.17 us
  transfers between devices with their start and end apart: 10, of which 4 were waited for; matrix products, arithmetic and copies ran while one was open for 5% of the time, Pallas kernels for 0%

commit v1 on v0

v1 whole, which is shorter than its diff:
```python
import functools

import jax
import jax.numpy as jnp
from jax import lax
from jax.experimental import pallas as pl
from jax.experimental.pallas import tpu as pltpu
from jax.sharding import PartitionSpec as P

K = 100
CL_GRP = 4
ITERS = 2
temper = 16.0

GROUPS = 32
CAP = 40
WINDOW = CAP + 8
HEAD = 32
LANES = 128
CHUNKS = 6
SEND_ROWS = 256
ZS = 8
OWN = 25
BLOCK = 32
PACK = 160
HALF = ZS * BLOCK
ITEMS = GROUPS * CAP
STEP = 256
f32 = jnp.float32
bf16 = jnp.bfloat16

ON_CHIP = pl.BlockSpec(memory_space=pltpu.VMEM)
SCALARS = pl.BlockSpec(memory_space=pltpu.SMEM)


def iota(shape, axis):
    return lax.broadcasted_iota(jnp.int32, shape, axis)


def chunk(i):
    return slice(i * LANES, (i + 1) * LANES)


def to_column(row, rows):
    shape = (rows, LANES)
    return jnp.sum(jnp.where(iota(shape, 0) == iota(shape, 1), row, 0.0), axis=1, keepdims=True)


def to_row(column):
    shape = (column.shape[0], LANES)
    return jnp.sum(jnp.where(iota(shape, 0) == iota(shape, 1), column, 0.0), axis=0, keepdims=True)


def front_kernel(counts, offsets, me, labels, owner, rows, out, wide, tags):
    local = jnp.bitwise_and(owner[...], CL_GRP - 1).astype(f32) + 1.0
    local = to_column(local, LANES)
    square = (LANES, LANES)
    for q in range(labels.shape[0]):
        hit = jnp.where(iota(square, 0) == labels[q : q + 1, :], local, 0.0)
        column = to_column(jnp.sum(hit, axis=0, keepdims=True), LANES)
        tags[q * LANES : (q + 1) * LANES, :] = jnp.broadcast_to(column, square)
    total = rows.shape[0]
    tags[total:, :] = jnp.zeros_like(tags[total:, :])
    wide[:total, :] = rows[...].astype(f32)
    wide[total:, :] = jnp.zeros_like(wide[total:, :])
    head_base = jnp.bitwise_and(me[0], 3) * HEAD
    tail_base = jnp.bitwise_and(me[0], 15) * (CAP - HEAD)

    def one(g, carry):
        first = offsets[0, g]
        count = counts[0, g]
        window = pl.ds(pl.multiple_of(first - jnp.bitwise_and(first, 7), 8), WINDOW)
        back = WINDOW - jnp.bitwise_and(first, 7)
        picked = pltpu.roll(wide[window, :], back, 0)[:CAP]
        picked = jnp.where(iota((CAP, 1), 0) < count, picked, 0.0)
        for i in range(CHUNKS):
            out[g, i * HEAD : (i + 1) * HEAD, :] = picked[:HEAD, chunk(i)].astype(bf16)
        for q in range(CHUNKS // 2):
            both = jnp.concatenate([picked[HEAD:, chunk(2 * q)], picked[HEAD:, chunk(2 * q + 1)]], axis=0)
            start = CHUNKS * HEAD + 16 * q
            out[g, start : start + 16, :] = both.astype(bf16)
        tag = pltpu.roll(tags[window, :], back, 0)[:CAP]
        sub, lane = iota((CAP, LANES), 0), iota((CAP, LANES), 1)
        place = jnp.where(sub < HEAD, sub + head_base, sub - HEAD + tail_base)
        tag = jnp.where((lane == place) & (sub < count), tag, 0.0)
        head = jnp.sum(tag[:HEAD], axis=0, keepdims=True)
        tail = jnp.sum(tag[HEAD:], axis=0, keepdims=True)
        which = iota((16, LANES), 0)
        tile = jnp.where(which == 0, head, jnp.where(which == 1, tail, 0.0))
        out[g, SEND_ROWS - 16 :, :] = tile.astype(bf16)
        return carry

    lax.fori_loop(0, GROUPS, one, 0, unroll=4)


def front(counts, offsets, me, labels, owner, rows):
    spare = rows.shape[0] + WINDOW
    return pl.pallas_call(
        front_kernel,
        out_shape=jax.ShapeDtypeStruct((GROUPS, SEND_ROWS, LANES), bf16),
        in_specs=[SCALARS, SCALARS, SCALARS, ON_CHIP, ON_CHIP, ON_CHIP],
        out_specs=ON_CHIP,
        scratch_shapes=[pltpu.VMEM((spare, rows.shape[1]), f32), pltpu.VMEM((spare, LANES), f32)],
        compiler_params=pltpu.CompilerParams(vmem_limit_bytes=24 * 2**20),
        name="front",
    )(counts, offsets, me, labels.reshape(-1, LANES), owner.reshape(1, -1), rows)


def pack_rows(pieces, lasts):
    parts = [jnp.concatenate([pieces[2 * q], pieces[2 * q + 1]], axis=0) for q in range(CHUNKS // 2)]
    which = iota((16, LANES), 0)
    end = jnp.zeros((16, LANES), f32)
    for i in range(CHUNKS):
        end = jnp.where(which == i, lasts[i], end)
    return parts, end


def pack_kernel(rows, out):
    wide = rows[...].astype(f32)
    pieces = [wide[:24, chunk(i)] for i in range(CHUNKS)]
    lasts = [wide[24:25, chunk(i)] for i in range(CHUNKS)]
    parts, end = pack_rows(pieces, lasts)
    for q in range(CHUNKS // 2):
        out[0, 48 * q : 48 * q + 48, :] = parts[q].astype(bf16)
    out[0, 144:, :] = end.astype(bf16)


def pack(rows):
    return pl.pallas_call(
        pack_kernel,
        out_shape=jax.ShapeDtypeStruct((1, PACK, LANES), bf16),
        in_specs=[ON_CHIP],
        out_specs=ON_CHIP,
        compiler_params=pltpu.CompilerParams(vmem_limit_bytes=4 * 2**20),
        name="pack",
    )(rows)


def sweep_kernel(arrived, mine, theirs, send, keep, items, panel, weights, sums):
    def head(s, carry):
        for i in range(CHUNKS):
            items[pl.ds(pl.multiple_of(s * HEAD, HEAD), HEAD), chunk(i)] = arrived[s, i * HEAD : (i + 1) * HEAD, :]
        return carry

    lax.fori_loop(0, GROUPS, head, 0, unroll=4)

    def tail(u, carry):
        rows = pl.ds(pl.multiple_of(GROUPS * HEAD + 16 * u, 16), 16)
        for q in range(CHUNKS // 2):
            start = CHUNKS * HEAD + 16 * q
            even = arrived[2 * u, start : start + 16, :].astype(f32)
            odd = arrived[2 * u + 1, start : start + 16, :].astype(f32)
            items[rows, chunk(2 * q)] = jnp.concatenate([even[:8], odd[:8]], axis=0).astype(bf16)
            items[rows, chunk(2 * q + 1)] = jnp.concatenate([even[8:], odd[8:]], axis=0).astype(bf16)
        return carry

    lax.fori_loop(0, GROUPS // 2, tail, 0, unroll=4)

    def tag_tile(s):
        return arrived[s, SEND_ROWS - 16 :, :].astype(f32)[:8]

    pieces = []
    for u in range(GROUPS // 4):
        tile = sum(tag_tile(4 * u + i) for i in range(4))
        pieces.append(tile[0:1])
    for v in range(GROUPS // 16):
        tile = sum(tag_tile(16 * v + i) for i in range(16))
        pieces.append(tile[1:2])
    tags = jnp.concatenate(pieces, axis=1) - 1.0

    lengths = []
    for half, source in enumerate((mine, theirs)):
        for z in range(ZS):
            start = half * HALF + z * BLOCK
            end = source[z, 144:, :].astype(f32)[:8]
            square = jnp.zeros((BLOCK, LANES), f32)
            for q in range(CHUNKS // 2):
                part = source[z, 48 * q : 48 * q + 48, :].astype(f32)
                for i in (2 * q, 2 * q + 1):
                    low = 24 * (i % 2)
                    last = jnp.where(iota((8, LANES), 0) == 0, end[i : i + 1], 0.0)
                    piece = jnp.concatenate([part[low : low + 24], last], axis=0)
                    square = square + piece * piece
                    panel[start : start + BLOCK, chunk(i)] = piece.astype(bf16)
            lengths.append(jnp.sum(square, axis=1, keepdims=True))
    lengths = jnp.concatenate(lengths, axis=0) * (1.0 / temper)

    part_rows = HALF // CL_GRP
    real = (iota((part_rows, 1), 0) % BLOCK) < OWN
    totals = [jnp.zeros((part_rows, LANES), f32) for _ in range(2 * CL_GRP)]
    for j in range(ITEMS // STEP):
        columns = slice(j * STEP, (j + 1) * STEP)
        product = lax.dot_general(
            panel[...], items[columns, :], (((1,), (1,)), ((), ())), preferred_element_type=f32
        )
        logits = product * (2.0 / temper) - lengths
        tag = tags[:, columns]
        picked = []
        for half in range(2):
            rows = [
                logits[half * HALF + c * part_rows : half * HALF + (c + 1) * part_rows]
                for c in range(CL_GRP)
            ]
            chosen = rows[0]
            for c in range(1, CL_GRP):
                chosen = jnp.where(tag == c, rows[c], chosen)
            picked.append(jnp.where(real, chosen, -3e38))
        highest = jnp.maximum(
            jnp.max(picked[0], axis=0, keepdims=True), jnp.max(picked[1], axis=0, keepdims=True)
        )
        exponent = [jnp.exp(p - highest) for p in picked]
        scale = 1.0 / (
            jnp.sum(exponent[0], axis=0, keepdims=True) + jnp.sum(exponent[1], axis=0, keepdims=True)
        )
        for half in range(2):
            weight = exponent[half] * scale
            for c in range(CL_GRP):
                own = jnp.where(tag == c, weight, 0.0)
                start = half * HALF + c * part_rows
                weights[start : start + part_rows, columns] = own.astype(bf16)
                n = half * CL_GRP + c
                for i in range(STEP // LANES):
                    totals[n] = totals[n] + own[:, chunk(i)]

    for half, out in ((1, send), (0, keep)):
        sums[...] = jnp.dot(
            weights[half * HALF : (half + 1) * HALF, :], items[...], preferred_element_type=f32
        )
        for z in range(ZS):
            start = z * BLOCK
            end = jnp.zeros((8, LANES), f32)
            for i in range(CHUNKS):
                out[z, 24 * i : 24 * i + 24, :] = sums[start : start + 24, chunk(i)]
                end = jnp.where(iota((8, LANES), 0) == i, sums[start + 24 : start + 25, chunk(i)], end)
            block = totals[half * CL_GRP + z // 2][(z % 2) * BLOCK : (z % 2 + 1) * BLOCK]
            total = to_row(jnp.sum(block, axis=1, keepdims=True))
            out[z, 144:152, :] = jnp.where(iota((8, LANES), 0) == 6, total, end)
            out[z, 152:, :] = jnp.zeros((8, LANES), f32)


def sweep(arrived, mine, theirs):
    shape = jax.ShapeDtypeStruct((ZS, PACK, LANES), f32)
    return pl.pallas_call(
        sweep_kernel,
        out_shape=(shape, shape),
        in_specs=[ON_CHIP] * 3,
        out_specs=(ON_CHIP, ON_CHIP),
        scratch_shapes=[
            pltpu.VMEM((ITEMS, CHUNKS * LANES), bf16),
            pltpu.VMEM((2 * HALF, CHUNKS * LANES), bf16),
            pltpu.VMEM((2 * HALF, ITEMS), bf16),
            pltpu.VMEM((HALF, CHUNKS * LANES), f32),
        ],
        compiler_params=pltpu.CompilerParams(vmem_limit_bytes=32 * 2**20),
        name="sweep",
    )(arrived, mine, theirs)


def join_kernel(keep, received, out):
    which = iota((8, LANES), 0)
    for z in range(ZS):
        out[z, :144, :] = (keep[z, :144, :] + received[z, :144, :]).astype(bf16)
        end = keep[z, 144:152, :] + received[z, 144:152, :]
        rest = end - end.astype(bf16).astype(f32)
        end = jnp.where(which == 7, rest[6:7], end)
        out[z, 144:, :] = jnp.concatenate([end, jnp.zeros_like(end)], axis=0).astype(bf16)


def join(keep, received):
    return pl.pallas_call(
        join_kernel,
        out_shape=jax.ShapeDtypeStruct((ZS, PACK, LANES), bf16),
        in_specs=[ON_CHIP] * 2,
        out_specs=ON_CHIP,
        compiler_params=pltpu.CompilerParams(vmem_limit_bytes=8 * 2**20),
        name="join",
    )(keep, received)


def update_kernel(parts, prior, out, *copies):
    total = parts[0].astype(f32)
    for z in range(1, ZS):
        total = total + parts[z].astype(f32)
    end = total[144:152]
    weight = to_column(end[6:7] + end[7:8], BLOCK) + 1.0
    before = prior[...].astype(f32)
    pieces, lasts = [], []
    for i in range(CHUNKS):
        piece = (total[24 * i : 24 * i + 24] + before[:24, chunk(i)]) / weight[:24]
        last = (end[i : i + 1] + before[24:25, chunk(i)]) / weight[24:25]
        out[:24, chunk(i)] = piece
        out[24:25, chunk(i)] = last
        pieces.append(piece)
        lasts.append(last)
    if copies:
        parts, end = pack_rows(pieces, lasts)
        parts = [p.astype(bf16) for p in parts]
        end = end.astype(bf16)
        for z in range(ZS):
            for q in range(CHUNKS // 2):
                copies[0][z, 48 * q : 48 * q + 48, :] = parts[q]
            copies[0][z, 144:, :] = end


def update(parts, prior, last):
    out_shape = [jax.ShapeDtypeStruct((OWN, CHUNKS * LANES), f32)]
    if not last:
        out_shape.append(jax.ShapeDtypeStruct((ZS, PACK, LANES), bf16))
    return pl.pallas_call(
        update_kernel,
        out_shape=out_shape,
        in_specs=[ON_CHIP] * 2,
        out_specs=[ON_CHIP] * len(out_shape),
        compiler_params=pltpu.CompilerParams(vmem_limit_bytes=8 * 2**20),
        name="update",
    )(parts, prior)


def shards(passages, labels, send_counts, send_offsets, owner_slot, centroids):
    members = lax.axis_size("member")
    along_z = [[m for m in range(members) if m % 2 == core] for core in range(2)]
    cores = [(m, m ^ 1) for m in range(members)]
    me = lax.axis_index("group").reshape(1).astype(jnp.int32)

    outgoing = front(send_counts, send_offsets, me, labels, owner_slot, passages)
    arrived = lax.all_to_all(outgoing, "group", split_axis=0, concat_axis=0, tiled=True)
    mine = lax.all_gather(pack(centroids), "member", axis=0, tiled=True, axis_index_groups=along_z)
    theirs = lax.ppermute(mine, "member", cores)
    prior = centroids
    for turn in range(ITERS):
        send, keep = sweep(arrived, mine, theirs)
        received = lax.ppermute(send, "member", cores)
        parts = lax.all_to_all(
            join(keep, received), "member", split_axis=0, concat_axis=0, tiled=True, axis_index_groups=along_z
        )
        last = turn == ITERS - 1
        prior, *copies = update(parts, prior, last)
        if not last:
            mine = lax.all_to_all(
                copies[0], "member", split_axis=0, concat_axis=0, tiled=True, axis_index_groups=along_z
            )
            theirs = lax.ppermute(mine, "member", cores)
    return prior


def solution(mesh):
    spec = P(("group", "member"))
    rows = P(("group", "member"), None)
    return jax.shard_map(
        shards,
        mesh=mesh,
        in_specs=(rows, spec, rows, rows, P(), rows),
        out_specs=rows,
        check_vma=False,
    )
```

time: 298 us -> 144 us (0.48); the launches traced: 294 us -> 144 us
  blocking collectives: 164 us -> 79.2 us
  local copies, waits for them, and re-layouts: 39.3 us -> 5.39 us
  other arithmetic: 25.3 us -> 0 us
  matrix products: 12.8 us -> 0 us
  Pallas kernels: 0 us -> 10.2 us
  starting transfers between devices: 37.6 us -> 29.6 us
  waiting for transfers between devices: 14.6 us -> 19 us
    unnamed x2 -> x0, blocking collectives: 67.7 us -> none
    all_to_all x0 -> x3, blocking collectives: none -> 52.2 us  [the longest x2 38.7 us: shards(): lax.all_to_all(join(keep, received), 'member', split_axis=0, concat_axis=...]
    psum x2 -> x0, blocking collectives: 46 us -> none  [shards(): totals_all = lax.psum(totals, 'member')]
    all_gather x2 -> x1, blocking collectives: 50.3 us -> 27 us  [shards(): lax.all_gather(pack(centroids), 'member', axis=0, tiled=True, axis_index_...]
    unnamed x8 -> x0, starting transfers between devices: 20.1 us -> none
    ppermute x0 -> x4, starting transfers between devices: none -> 19 us  [the longest x2 12.2 us: shards(): theirs = lax.ppermute(mine, 'member', cores)]
    dot_general x4 -> x0, matrix products: 12.8 us -> none  [the longest x2 7.74 us: shards(): lax.dot_general(panel_rows, arrived, (((1,), (1,)), ((), ())), preferred_...]
    all_to_all x1 -> x0, starting transfers between devices: 10.6 us -> none  [shards(): lax.all_to_all(slot_tags, 'group', split_axis=0, concat_axis=0, tiled=True)]
  transfers between devices with their start and end apart: 10 -> 5, of which waited for: 4 -> 5; matrix products, arithmetic and copies ran while one was open for 5% -> 0% of each run, Pallas kernels for 0% -> 0%
where the time goes in v1:
time: 144 us
  blocking collectives  79.2 us (55%)
  starting transfers between devices  29.6 us (21%)
  waiting for transfers between devices  19 us (13%)
  Pallas kernels  10.2 us (7%)
  local copies, waits for them, and re-layouts  5.39 us (4%)
    all_to_all x2, blocking collectives, shards(): lax.all_to_all(join(keep, received), 'member', split_axis=0, concat_axis=...  38.7 us
    all_gather x1, blocking collectives, shards(): lax.all_gather(pack(centroids), 'member', axis=0, tiled=True, axis_index_...  27 us
    all_to_all x1, blocking collectives, shards(): lax.all_to_all(copies[0], 'member', split_axis=0, concat_axis=0, tiled=Tr...  13.4 us
    all_to_all x1, waiting for transfers between devices, shards(): lax.all_to_all(outgoing, 'group', split_axis=0, concat_axis=0, tiled=True)  13.1 us
    ppermute x2, starting transfers between devices, shards(): theirs = lax.ppermute(mine, 'member', cores)  12.2 us
    all_to_all x1, starting transfers between devices, shards(): lax.all_to_all(outgoing, 'group', split_axis=0, concat_axis=0, tiled=True)  10.6 us
    ppermute x2, starting transfers between devices, shards(): received = lax.ppermute(send, 'member', cores)  6.82 us
    pallas_call x2, Pallas kernels, sweep(): pl.pallas_call(sweep_kernel, out_shape=(shape, shape), in_specs=[ON_CHIP]...  6.77 us
  transfers between devices with their start and end apart: 5, of which 5 were waited for; matrix products, arithmetic and copies ran while one was open for 0% of the time, Pallas kernels for 0%

profile of v1, /device:TPU:1, one launch (start us, length us, event | category | flops | bytes accessed | tf_op | source)
XLA Modules:
  0.0 143.5 jit_solution(17969542917659230977)
XLA Ops:
  0.0 0.0 copy-start.1
  0.0 1.4 copy-done.1
  1.4 0.7 copy-done.3
  2.1 0.0 copy-start.4
  2.1 0.7 copy-done.4
  2.8 0.0 copy-start.5
  2.8 0.7 copy-done.5
  3.4 0.7 copy-done.6
  4.1 2.5 %front.1 = bf16[32,256,128]{2,1,0:T(8,128)(2,1)S(1)} custom-call(s32[1,32]{1,0:T(1,128)S(1)} %copy-done.4, s32[1,32]{1,0:T(1,128)S(1)} %copy-done.5, s32[1]{0:T(128)} %bitcast.me, s32[8,128]{1,0:T(8,128)S(1)} %bitcast.3, s32[1,128]{1,0:T(1,128)S(1)} %bitcast.4, bf16[1024,768]{1,0:T(8,128)(2,1)S(1)} %copy-done.1), custom_call_target="tpu_custom_call" | custom-call | tf_op jit(solution)/shard_map/front/pallas_call | solution.py:98
  6.5 0.0 copy-start
  6.5 1.3 copy-done
  7.9 10.6 %all-to-all-start = ((bf16[32,256,128]{2,1,0:T(8,128)(2,1)}), bf16[32,256,128]{2,1,0:T(8,128)(2,1)S(1)}, u32[]{:S(2)}, u32[]{:S(2)}) async-start(bf16[32,256,128]{2,1,0:T(8,128)(2,1)} %copy-done), calls=%async_computation | async-start | bytes 4194304 | tf_op jit(solution)/shard_map/all_to_all | solution.py:326
  18.5 0.0 copy-done.2
  18.5 27.0 %all_gather.3.mine = bf16[8,160,128]{2,1,0:T(8,128)(2,1)S(1)} all-gather(bf16[1,160,128]{2,1,0:T(8,128)(2,1)S(1)} %pack.1), channel_id=1, replica_groups={{0,2,4,6,8,10,12,14},{1,3,5,7,9,11,13,15},{16,18,20,22,24,26,28,30},{17..., dimensions={0}, use_global_device_ids=true | all-gather | bytes 368640 | tf_op jit(solution)/shard_map/all_gather | solution.py:327
  45.5 7.1 %collective-permute-start = (bf16[8,160,128]{2,1,0:T(8,128)(2,1)S(1)}, bf16[8,160,128]{2,1,0:T(8,128)(2,1)S(1)}, u32[]{:S(2)}, u32[]{:S(2)}) collective-permute-start(bf16[8,160,128]{2,1,0:T(8,128)(2,1)S(1)} %all_gather.3.mine), channel_id=1, source_target_pairs={{0,1},{1,0},{2,3},{3,2},{4,5},{5,4},{6,7},{7,6},{8,9},{9,8},{10,11... | collective-permute-start | bytes 983048 | tf_op jit(solution)/shard_map/ppermute | solution.py:328
  52.7 1.2 collective-permute-done.theirs
  53.9 13.1 %all-to-all-done.arrived = bf16[32,256,128]{2,1,0:T(8,128)(2,1)S(1)} async-done(((bf16[32,256,128]{2,1,0:T(8,128)(2,1)}), bf16[32,256,128]{2,1,0:T(8,128)(2,1)S(1)}, u32[]{:S(2)}, u32[]{:S(2)}) %all-to-all-start) | async-done | bytes 2097184 | tf_op jit(solution)/shard_map/all_to_all | solution.py:326
  67.0 3.4 %sweep.2 = (f32[8,160,128]{2,1,0:T(8,128)S(1)}, f32[8,160,128]{2,1,0:T(8,128)S(1)}) custom-call(bf16[32,256,128]{2,1,0:T(8,128)(2,1)S(1)} %all-to-all-done.arrived, bf16[8,160,128]{2,1,0:T(8,128)(2,1)S(1)} %all_gather.3.mine, bf16[8,160,128]{2,1,0:T(8,128)(2,1)S(1)} %collective-permute-done.theirs), custom_call_target="tpu_custom_call" | custom-call | tf_op jit(solution)/shard_map/sweep/pallas_call | solution.py:243
  70.4 4.5 %collective-permute-start.1 = (f32[8,160,128]{2,1,0:T(8,128)S(1)}, f32[8,160,128]{2,1,0:T(8,128)S(1)}, u32[]{:S(2)}, u32[]{:S(2)}) collective-permute-start(f32[8,160,128]{2,1,0:T(8,128)S(1)} %get-tuple-element.12), channel_id=1, source_target_pairs={{0,1},{1,0},{2,3},{3,2},{4,5},{5,4},{6,7},{7,6},{8,9},{9,8},{10,11... | collective-permute-start | bytes 1966088 | tf_op jit(solution)/shard_map/ppermute | solution.py:332
  74.9 1.7 %collective-permute-done.1.received = f32[8,160,128]{2,1,0:T(8,128)S(1)} collective-permute-done((f32[8,160,128]{2,1,0:T(8,128)S(1)}, f32[8,160,128]{2,1,0:T(8,128)S(1)}, u32[]{:S(2)}, u32[]{:S(2)}) %collective-permute-start.1) | collective-permute-done | bytes 655392 | tf_op jit(solution)/shard_map/ppermute | solution.py:332
  76.6 0.1 join.2
  76.7 22.6 %all_to_all.20.parts = bf16[8,160,128]{2,1,0:T(8,128)(2,1)S(1)} all-to-all(bf16[8,160,128]{2,1,0:T(8,128)(2,1)S(1)} %join.2), channel_id=1, replica_groups={{0,2,4,6,8,10,12,14},{1,3,5,7,9,11,13,15},{16,18,20,22,24,26,28,30},{17..., dimensions={0} | all-to-all | bytes 655360 | tf_op jit(solution)/shard_map/all_to_all | solution.py:333
  99.3 0.1 update.2
  99.4 13.4 %all_to_all.21.mine = bf16[8,160,128]{2,1,0:T(8,128)(2,1)S(1)} all-to-all(bf16[8,160,128]{2,1,0:T(8,128)(2,1)S(1)} %get-tuple-element.13), channel_id=1, replica_groups={{0,2,4,6,8,10,12,14},{1,3,5,7,9,11,13,15},{16,18,20,22,24,26,28,30},{17..., dimensions={0} | all-to-all | bytes 655360 | tf_op jit(solution)/shard_map/all_to_all | solution.py:339
  112.9 5.1 %collective-permute-start.2 = (bf16[8,160,128]{2,1,0:T(8,128)(2,1)S(1)}, bf16[8,160,128]{2,1,0:T(8,128)(2,1)S(1)}, u32[]{:S(2)}, u32[]{:S(2)}) collective-permute-start(bf16[8,160,128]{2,1,0:T(8,128)(2,1)S(1)} %all_to_all.21.mine), channel_id=1, source_target_pairs={{0,1},{1,0},{2,3},{3,2},{4,5},{5,4},{6,7},{7,6},{8,9},{9,8},{10,11... | collective-permute-start | bytes 983048 | tf_op jit(solution)/shard_map/ppermute | solution.py:342
  117.9 1.2 collective-permute-done.2.theirs
  119.2 3.4 %sweep.3 = (f32[8,160,128]{2,1,0:T(8,128)S(1)}, f32[8,160,128]{2,1,0:T(8,128)S(1)}) custom-call(bf16[32,256,128]{2,1,0:T(8,128)(2,1)S(1)} %all-to-all-done.arrived, bf16[8,160,128]{2,1,0:T(8,128)(2,1)S(1)} %all_to_all.21.mine, bf16[8,160,128]{2,1,0:T(8,128)(2,1)S(1)} %collective-permute-done.2.theirs), custom_call_target="tpu_custom_call" | custom-call | tf_op jit(solution)/shard_map/sweep/pallas_call | solution.py:243
  122.6 2.3 %collective-permute-start.3 = (f32[8,160,128]{2,1,0:T(8,128)S(1)}, f32[8,160,128]{2,1,0:T(8,128)S(1)}, u32[]{:S(2)}, u32[]{:S(2)}) collective-permute-start(f32[8,160,128]{2,1,0:T(8,128)S(1)} %get-tuple-element.15), channel_id=1, source_target_pairs={{0,1},{1,0},{2,3},{3,2},{4,5},{5,4},{6,7},{7,6},{8,9},{9,8},{10,11... | collective-permute-start | bytes 1966088 | tf_op jit(solution)/shard_map/ppermute | solution.py:332
  124.9 1.7 %collective-permute-done.3.received = f32[8,160,128]{2,1,0:T(8,128)S(1)} collective-permute-done((f32[8,160,128]{2,1,0:T(8,128)S(1)}, f32[8,160,128]{2,1,0:T(8,128)S(1)}, u32[]{:S(2)}, u32[]{:S(2)}) %collective-permute-start.3) | collective-permute-done | bytes 655392 | tf_op jit(solution)/shard_map/ppermute | solution.py:332
  126.6 0.1 join.3
  126.6 16.1 %all_to_all.22.parts = bf16[8,160,128]{2,1,0:T(8,128)(2,1)S(1)} all-to-all(bf16[8,160,128]{2,1,0:T(8,128)(2,1)S(1)} %join.3), channel_id=1, replica_groups={{0,2,4,6,8,10,12,14},{1,3,5,7,9,11,13,15},{16,18,20,22,24,26,28,30},{17..., dimensions={0} | all-to-all | bytes 655360 | tf_op jit(solution)/shard_map/all_to_all | solution.py:333
  142.8 0.7 update.3
  (4 shorter events, 0.0 us)
Async XLA Ops:
  0.0 1.4 copy-start.1
  1.4 0.7 copy-start.3
  2.1 0.7 copy-start.4
  2.8 0.7 copy-start.5
  3.4 0.7 copy-start.6
  6.5 1.3 copy-start
  7.9 10.6 %copy-start.2 = (bf16[25,768]{1,0:T(8,128)(2,1)S(1)}, bf16[25,768]{1,0:T(8,128)(2,1)}, u32[]{:S(2)}) copy-start(bf16[25,768]{1,0:T(8,128)(2,1)} %prior.1) | copy-start | bytes 115204
  7.9 59.1 %all-to-all-start = ((bf16[32,256,128]{2,1,0:T(8,128)(2,1)}), bf16[32,256,128]{2,1,0:T(8,128)(2,1)S(1)}, u32[]{:S(2)}, u32[]{:S(2)}) async-start(bf16[32,256,128]{2,1,0:T(8,128)(2,1)} %copy-done), calls=%async_computation | async-start | bytes 4194304 | tf_op jit(solution)/shard_map/all_to_all | solution.py:326
  45.5 8.3 %collective-permute-start = (bf16[8,160,128]{2,1,0:T(8,128)(2,1)S(1)}, bf16[8,160,128]{2,1,0:T(8,128)(2,1)S(1)}, u32[]{:S(2)}, u32[]{:S(2)}) collective-permute-start(bf16[8,160,128]{2,1,0:T(8,128)(2,1)S(1)} %all_gather.3.mine), channel_id=1, source_target_pairs={{0,1},{1,0},{2,3},{3,2},{4,5},{5,4},{6,7},{7,6},{8,9},{9,8},{10,11... | collective-permute-start | bytes 983048 | tf_op jit(solution)/shard_map/ppermute | solution.py:328
  70.4 6.3 %collective-permute-start.1 = (f32[8,160,128]{2,1,0:T(8,128)S(1)}, f32[8,160,128]{2,1,0:T(8,128)S(1)}, u32[]{:S(2)}, u32[]{:S(2)}) collective-permute-start(f32[8,160,128]{2,1,0:T(8,128)S(1)} %get-tuple-element.12), channel_id=1, source_target_pairs={{0,1},{1,0},{2,3},{3,2},{4,5},{5,4},{6,7},{7,6},{8,9},{9,8},{10,11... | collective-permute-start | bytes 1966088 | tf_op jit(solution)/shard_map/ppermute | solution.py:332
  112.9 6.3 %collective-permute-start.2 = (bf16[8,160,128]{2,1,0:T(8,128)(2,1)S(1)}, bf16[8,160,128]{2,1,0:T(8,128)(2,1)S(1)}, u32[]{:S(2)}, u32[]{:S(2)}) collective-permute-start(bf16[8,160,128]{2,1,0:T(8,128)(2,1)S(1)} %all_to_all.21.mine), channel_id=1, source_target_pairs={{0,1},{1,0},{2,3},{3,2},{4,5},{5,4},{6,7},{7,6},{8,9},{9,8},{10,11... | collective-permute-start | bytes 983048 | tf_op jit(solution)/shard_map/ppermute | solution.py:342
  122.6 4.0 %collective-permute-start.3 = (f32[8,160,128]{2,1,0:T(8,128)S(1)}, f32[8,160,128]{2,1,0:T(8,128)S(1)}, u32[]{:S(2)}, u32[]{:S(2)}) collective-permute-start(f32[8,160,128]{2,1,0:T(8,128)S(1)} %get-tuple-element.15), channel_id=1, source_target_pairs={{0,1},{1,0},{2,3},{3,2},{4,5},{5,4},{6,7},{7,6},{8,9},{9,8},{10,11... | collective-permute-start | bytes 1966088 | tf_op jit(solution)/shard_map/ppermute | solution.py:332

commit v2 on v1

--- a/solution.py
+++ b/solution.py
@@ -18,11 +18,14 @@
 HEAD = 32
 LANES = 128
 CHUNKS = 6
-SEND_ROWS = 256
+TAG_ROWS = 8
+SEND_ROWS = 240 + TAG_ROWS
+ROW_PARTS = 4
+OUT_PARTS = 4
 ZS = 8
 OWN = 25
 BLOCK = 32
-PACK = 160
+PACK = 152
 HALF = ZS * BLOCK
 ITEMS = GROUPS * CAP
 STEP = 256
@@ -30,6 +33,7 @@
 bf16 = jnp.bfloat16
 
 ON_CHIP = pl.BlockSpec(memory_space=pltpu.VMEM)
+FAR = pl.BlockSpec(memory_space=pltpu.HBM)
 SCALARS = pl.BlockSpec(memory_space=pltpu.SMEM)
 
 
@@ -51,7 +55,27 @@
     return jnp.sum(jnp.where(iota(shape, 0) == iota(shape, 1), column, 0.0), axis=0, keepdims=True)
 
 
-def front_kernel(counts, offsets, me, labels, owner, rows, out, wide, tags):
+def front_kernel(me, counts_in, offsets_in, labels_in, owner_in, rows_in, out_far, *scratch):
+    counts, offsets, labels, owner, rows, wide, tags, out, small_done, rows_done, out_done = scratch
+    total = rows.shape[0]
+    part = total // ROW_PARTS
+    small = [
+        pltpu.make_async_copy(source, target, small_done.at[i])
+        for i, (source, target) in enumerate(
+            ((labels_in, labels), (owner_in, owner), (counts_in, counts), (offsets_in, offsets))
+        )
+    ]
+    for copy in small:
+        copy.start()
+    parts = []
+    for i in range(ROW_PARTS):
+        where = pl.ds(i * part, part)
+        parts.append(pltpu.make_async_copy(rows_in.at[where], rows.at[where], rows_done.at[i]))
+        parts[-1].start()
+    tags[total:, :] = jnp.zeros_like(tags[total:, :])
+    wide[total:, :] = jnp.zeros_like(wide[total:, :])
+    small[0].wait()
+    small[1].wait()
     local = jnp.bitwise_and(owner[...], CL_GRP - 1).astype(f32) + 1.0
     local = to_column(local, LANES)
     square = (LANES, LANES)
@@ -59,10 +83,11 @@
         hit = jnp.where(iota(square, 0) == labels[q : q + 1, :], local, 0.0)
         column = to_column(jnp.sum(hit, axis=0, keepdims=True), LANES)
         tags[q * LANES : (q + 1) * LANES, :] = jnp.broadcast_to(column, square)
-    total = rows.shape[0]
-    tags[total:, :] = jnp.zeros_like(tags[total:, :])
-    wide[:total, :] = rows[...].astype(f32)
-    wide[total:, :] = jnp.zeros_like(wide[total:, :])
+    for i in range(ROW_PARTS):
+        parts[i].wait()
+        wide[i * part : (i + 1) * part, :] = rows[i * part : (i + 1) * part, :].astype(f32)
+    small[2].wait()
+    small[3].wait()
     head_base = jnp.bitwise_and(me[0], 3) * HEAD
     tail_base = jnp.bitwise_and(me[0], 15) * (CAP - HEAD)
 
@@ -85,31 +110,53 @@
         tag = jnp.where((lane == place) & (sub < count), tag, 0.0)
         head = jnp.sum(tag[:HEAD], axis=0, keepdims=True)
         tail = jnp.sum(tag[HEAD:], axis=0, keepdims=True)
-        which = iota((16, LANES), 0)
+        which = iota((TAG_ROWS, LANES), 0)
         tile = jnp.where(which == 0, head, jnp.where(which == 1, tail, 0.0))
-        out[g, SEND_ROWS - 16 :, :] = tile.astype(bf16)
+        out[g, SEND_ROWS - TAG_ROWS :, :] = tile.astype(bf16)
         return carry
 
-    lax.fori_loop(0, GROUPS, one, 0, unroll=4)
-
-
-def front(counts, offsets, me, labels, owner, rows):
+    batch = GROUPS // OUT_PARTS
+    sent = []
+    for i in range(OUT_PARTS):
+        lax.fori_loop(i * batch, (i + 1) * batch, one, 0, unroll=4)
+        where = pl.ds(i * batch, batch)
+        sent.append(pltpu.make_async_copy(out.at[where], out_far.at[where], out_done.at[i]))
+        sent[-1].start()
+    for copy in sent:
+        copy.wait()
+
+
+def front(me, counts, offsets, labels, owner, rows):
     spare = rows.shape[0] + WINDOW
+    labels = labels.reshape(-1, LANES)
+    owner = owner.reshape(1, -1)
+    sent = (GROUPS, SEND_ROWS, LANES)
     return pl.pallas_call(
         front_kernel,
-        out_shape=jax.ShapeDtypeStruct((GROUPS, SEND_ROWS, LANES), bf16),
-        in_specs=[SCALARS, SCALARS, SCALARS, ON_CHIP, ON_CHIP, ON_CHIP],
-        out_specs=ON_CHIP,
-        scratch_shapes=[pltpu.VMEM((spare, rows.shape[1]), f32), pltpu.VMEM((spare, LANES), f32)],
-        compiler_params=pltpu.CompilerParams(vmem_limit_bytes=24 * 2**20),
+        out_shape=jax.ShapeDtypeStruct(sent, bf16),
+        in_specs=[SCALARS] + [FAR] * 5,
+        out_specs=FAR,
+        scratch_shapes=[
+            pltpu.SMEM(counts.shape, jnp.int32),
+            pltpu.SMEM(offsets.shape, jnp.int32),
+            pltpu.VMEM(labels.shape, jnp.int32),
+            pltpu.VMEM(owner.shape, jnp.int32),
+            pltpu.VMEM(rows.shape, bf16),
+            pltpu.VMEM((spare, rows.shape[1]), f32),
+            pltpu.VMEM((spare, LANES), f32),
+            pltpu.VMEM(sent, bf16),
+            pltpu.SemaphoreType.DMA((4,)),
+            pltpu.SemaphoreType.DMA((ROW_PARTS,)),
+            pltpu.SemaphoreType.DMA((OUT_PARTS,)),
+        ],
         name="front",
-    )(counts, offsets, me, labels.reshape(-1, LANES), owner.reshape(1, -1), rows)
+    )(me, counts, offsets, labels, owner, rows)
 
 
 def pack_rows(pieces, lasts):
     parts = [jnp.concatenate([pieces[2 * q], pieces[2 * q + 1]], axis=0) for q in range(CHUNKS // 2)]
-    which = iota((16, LANES), 0)
-    end = jnp.zeros((16, LANES), f32)
+    which = iota((8, LANES), 0)
+    end = jnp.zeros((8, LANES), f32)
     for i in range(CHUNKS):
         end = jnp.where(which == i, lasts[i], end)
     return parts, end
@@ -136,7 +183,7 @@
     )(rows)
 
 
-def sweep_kernel(arrived, mine, theirs, send, keep, items, panel, weights, sums):
+def unpack_items(arrived, items, tags):
     def head(s, carry):
         for i in range(CHUNKS):
             items[pl.ds(pl.multiple_of(s * HEAD, HEAD), HEAD), chunk(i)] = arrived[s, i * HEAD : (i + 1) * HEAD, :]
@@ -157,7 +204,7 @@
     lax.fori_loop(0, GROUPS // 2, tail, 0, unroll=4)
 
     def tag_tile(s):
-        return arrived[s, SEND_ROWS - 16 :, :].astype(f32)[:8]
+        return arrived[s, SEND_ROWS - TAG_ROWS :, :].astype(f32)
 
     pieces = []
     for u in range(GROUPS // 4):
@@ -166,16 +213,25 @@
     for v in range(GROUPS // 16):
         tile = sum(tag_tile(16 * v + i) for i in range(16))
         pieces.append(tile[1:2])
-    tags = jnp.concatenate(pieces, axis=1) - 1.0
+    tags[...] = jnp.concatenate(pieces, axis=1) - 1.0
+
+
+def sweep_kernel(first, core, *refs):
+    if first:
+        arrived, blocks, send, keep, items, tags, panel, weights, sums = refs
+        unpack_items(arrived, items, tags)
+    else:
+        items, tags, blocks, send, keep, panel, weights, sums = refs
 
     lengths = []
-    for half, source in enumerate((mine, theirs)):
+    for half in range(2):
         for z in range(ZS):
             start = half * HALF + z * BLOCK
-            end = source[z, 144:, :].astype(f32)[:8]
+            source = 2 * z + jnp.bitwise_xor(core[0], half)
+            end = blocks[source, 144:, :].astype(f32)
             square = jnp.zeros((BLOCK, LANES), f32)
             for q in range(CHUNKS // 2):
-                part = source[z, 48 * q : 48 * q + 48, :].astype(f32)
+                part = blocks[source, 48 * q : 48 * q + 48, :].astype(f32)
                 for i in (2 * q, 2 * q + 1):
                     low = 24 * (i % 2)
                     last = jnp.where(iota((8, LANES), 0) == 0, end[i : i + 1], 0.0)
@@ -235,25 +291,27 @@
             block = totals[half * CL_GRP + z // 2][(z % 2) * BLOCK : (z % 2 + 1) * BLOCK]
             total = to_row(jnp.sum(block, axis=1, keepdims=True))
             out[z, 144:152, :] = jnp.where(iota((8, LANES), 0) == 6, total, end)
-            out[z, 152:, :] = jnp.zeros((8, LANES), f32)
-
-
-def sweep(arrived, mine, theirs):
-    shape = jax.ShapeDtypeStruct((ZS, PACK, LANES), f32)
+
+
+def sweep(core, passages, blocks, first):
+    sums = jax.ShapeDtypeStruct((ZS, PACK, LANES), f32)
+    out_shape = [sums, sums]
+    if first:
+        out_shape.append(jax.ShapeDtypeStruct((ITEMS, CHUNKS * LANES), bf16))
+        out_shape.append(jax.ShapeDtypeStruct((1, ITEMS), f32))
     return pl.pallas_call(
-        sweep_kernel,
-        out_shape=(shape, shape),
-        in_specs=[ON_CHIP] * 3,
-        out_specs=(ON_CHIP, ON_CHIP),
+        functools.partial(sweep_kernel, first),
+        out_shape=out_shape,
+        in_specs=[SCALARS] + [ON_CHIP] * (len(passages) + 1),
+        out_specs=[ON_CHIP] * len(out_shape),
         scratch_shapes=[
-            pltpu.VMEM((ITEMS, CHUNKS * LANES), bf16),
             pltpu.VMEM((2 * HALF, CHUNKS * LANES), bf16),
             pltpu.VMEM((2 * HALF, ITEMS), bf16),
             pltpu.VMEM((HALF, CHUNKS * LANES), f32),
         ],
         compiler_params=pltpu.CompilerParams(vmem_limit_bytes=32 * 2**20),
         name="sweep",
-    )(arrived, mine, theirs)
+    )(core, *passages, blocks)
 
 
 def join_kernel(keep, received, out):
@@ -263,7 +321,7 @@
         end = keep[z, 144:152, :] + received[z, 144:152, :]
         rest = end - end.astype(bf16).astype(f32)
         end = jnp.where(which == 7, rest[6:7], end)
-        out[z, 144:, :] = jnp.concatenate([end, jnp.zeros_like(end)], axis=0).astype(bf16)
+        out[z, 144:, :] = end.astype(bf16)
 
 
 def join(keep, received):
@@ -277,7 +335,7 @@
     )(keep, received)
 
 
-def update_kernel(parts, prior, out, *copies):
+def update_kernel(parts, prior, out, *packed):
     total = parts[0].astype(f32)
     for z in range(1, ZS):
         total = total + parts[z].astype(f32)
@@ -292,20 +350,17 @@
         out[24:25, chunk(i)] = last
         pieces.append(piece)
         lasts.append(last)
-    if copies:
+    if packed:
         parts, end = pack_rows(pieces, lasts)
-        parts = [p.astype(bf16) for p in parts]
-        end = end.astype(bf16)
-        for z in range(ZS):
-            for q in range(CHUNKS // 2):
-                copies[0][z, 48 * q : 48 * q + 48, :] = parts[q]
-            copies[0][z, 144:, :] = end
+        for q in range(CHUNKS // 2):
+            packed[0][0, 48 * q : 48 * q + 48, :] = parts[q].astype(bf16)
+        packed[0][0, 144:, :] = end.astype(bf16)
 
 
 def update(parts, prior, last):
     out_shape = [jax.ShapeDtypeStruct((OWN, CHUNKS * LANES), f32)]
     if not last:
-        out_shape.append(jax.ShapeDtypeStruct((ZS, PACK, LANES), bf16))
+        out_shape.append(jax.ShapeDtypeStruct((1, PACK, LANES), bf16))
     return pl.pallas_call(
         update_kernel,
         out_shape=out_shape,
@@ -321,25 +376,22 @@
     along_z = [[m for m in range(members) if m % 2 == core] for core in range(2)]
     cores = [(m, m ^ 1) for m in range(members)]
     me = lax.axis_index("group").reshape(1).astype(jnp.int32)
-
-    outgoing = front(send_counts, send_offsets, me, labels, owner_slot, passages)
-    arrived = lax.all_to_all(outgoing, "group", split_axis=0, concat_axis=0, tiled=True)
-    mine = lax.all_gather(pack(centroids), "member", axis=0, tiled=True, axis_index_groups=along_z)
-    theirs = lax.ppermute(mine, "member", cores)
+    core = jnp.bitwise_and(lax.axis_index("member"), 1).reshape(1).astype(jnp.int32)
+
+    outgoing = front(me, send_counts, send_offsets, labels, owner_slot, passages)
+    passage_refs = [lax.all_to_all(outgoing, "group", split_axis=0, concat_axis=0, tiled=True)]
+    packed = pack(centroids)
     prior = centroids
     for turn in range(ITERS):
-        send, keep = sweep(arrived, mine, theirs)
+        blocks = lax.all_gather(packed, "member", axis=0, tiled=True)
+        send, keep, *unpacked = sweep(core, passage_refs, blocks, turn == 0)
+        passage_refs = unpacked or passage_refs
         received = lax.ppermute(send, "member", cores)
         parts = lax.all_to_all(
             join(keep, received), "member", split_axis=0, concat_axis=0, tiled=True, axis_index_groups=along_z
         )
-        last = turn == ITERS - 1
-        prior, *copies = update(parts, prior, last)
-        if not last:
-            mine = lax.all_to_all(
-                copies[0], "member", split_axis=0, concat_axis=0, tiled=True, axis_index_groups=along_z
-            )
-            theirs = lax.ppermute(mine, "member", cores)
+        prior, *packed = update(parts, prior, turn == ITERS - 1)
+        packed = packed[0] if packed else None
     return prior
 
 

time: 144 us -> 136 us (0.944)
  starting transfers between devices: 29.6 us -> 17.2 us
  waiting for transfers between devices: 19 us -> 25 us
  local copies, waits for them, and re-layouts: 5.39 us -> 0.01 us
  blocking collectives: 79.2 us -> 81.8 us
    all_gather x1 -> x2, blocking collectives: 27 us -> 43.3 us  [shards(): blocks = lax.all_gather(packed, 'member', axis=0, tiled=True)]
    all_to_all x1 -> x0, blocking collectives: 13.4 us -> none  [shards(): lax.all_to_all(copies[0], 'member', split_axis=0, concat_axis=0, tiled=Tr...]
    ppermute x2 -> x0, starting transfers between devices: 12.2 us -> none  [shards(): theirs = lax.ppermute(mine, 'member', cores)]
    all_to_all x1, waiting for transfers between devices: 13.1 us -> 21.4 us  [shards(): lax.all_to_all(outgoing, 'group', split_axis=0, concat_axis=0, tiled=True)]
    unnamed x14 -> x2, local copies, waits for them, and re-layouts: 5.39 us -> 0.01 us
    ppermute x2 -> x0, waiting for transfers between devices: 2.47 us -> none  [shards(): theirs = lax.ppermute(mine, 'member', cores)]
  transfers between devices with their start and end apart: 5 -> 3, of which waited for: 5 -> 3; matrix products, arithmetic and copies ran while one was open for 0% -> 0% of each run, Pallas kernels for 0% -> 0%
where the time goes in v2:
time: 136 us; the launch traced here: 135 us
  blocking collectives  81.8 us (60%)
  waiting for transfers between devices  25 us (18%)
  starting transfers between devices  17.2 us (13%)
  Pallas kernels  11.3 us (8%)
    all_gather x2, blocking collectives, shards(): blocks = lax.all_gather(packed, 'member', axis=0, tiled=True)  43.3 us
    all_to_all x2, blocking collectives, shards(): lax.all_to_all(join(keep, received), 'member', split_axis=0, concat_axis=...  38.4 us
    all_to_all x1, waiting for transfers between devices, shards(): lax.all_to_all(outgoing, 'group', split_axis=0, concat_axis=0, tiled=True)  21.4 us
    all_to_all x1, starting transfers between devices, shards(): lax.all_to_all(outgoing, 'group', split_axis=0, concat_axis=0, tiled=True)  10.6 us
    ppermute x2, starting transfers between devices, shards(): received = lax.ppermute(send, 'member', cores)  6.59 us
    pallas_call x2, Pallas kernels, sweep(): pl.pallas_call(functools.partial(sweep_kernel, first), out_shape=out_shap...  6.42 us
    pallas_call x1, Pallas kernels, front(): pl.pallas_call(front_kernel, out_shape=jax.ShapeDtypeStruct(sent, bf16),...  3.76 us
    ppermute x2, waiting for transfers between devices, shards(): received = lax.ppermute(send, 'member', cores)  3.53 us
  transfers between devices with their start and end apart: 3, of which 3 were waited for; matrix products, arithmetic and copies ran while one was open for 0% of the time, Pallas kernels for 0%

profile of v2, /device:TPU:1, one launch (start us, length us, event | category | flops | bytes accessed | tf_op | source)
XLA Modules:
  0.0 135.3 jit_solution(12662682371338037962)
XLA Ops:
  0.0 3.8 %front.1 = bf16[32,248,128]{2,1,0:T(8,128)(2,1)} custom-call(s32[1]{0:T(128)} %bitcast.1.me, s32[1,32]{1,0:T(1,128)} %counts_in.1, s32[1,32]{1,0:T(1,128)} %offsets_in.1, s32[8,128]{1,0:T(8,128)} %bitcast.4, s32[1,128]{1,0:T(1,128)} %bitcast.5, bf16[1024,768]{1,0:T(8,128)(2,1)} %rows_in.1), custom_call_target="tpu_custom_call" | custom-call | tf_op jit(solution)/shard_map/front/pallas_call | solution.py:134
  3.8 0.0 copy-start
  3.8 10.6 %all-to-all-start = ((bf16[32,248,128]{2,1,0:T(8,128)(2,1)}), bf16[32,248,128]{2,1,0:T(8,128)(2,1)S(1)}, u32[]{:S(2)}, u32[]{:S(2)}) async-start(bf16[32,248,128]{2,1,0:T(8,128)(2,1)} %front.1), calls=%async_computation | async-start | bytes 4063232 | tf_op jit(solution)/shard_map/all_to_all | solution.py:382
  14.4 0.0 copy-done
  14.5 25.7 %all_gather.6.refs_1_ = bf16[16,152,128]{2,1,0:T(8,128)(2,1)S(1)} all-gather(bf16[1,152,128]{2,1,0:T(8,128)(2,1)S(1)} %pack.1), channel_id=1, replica_groups=mesh['group'=32,'member'=16] {'member'}, dimensions={0}, use_global_device_ids=true | all-gather | bytes 661504 | tf_op jit(solution)/shard_map/all_gather | solution.py:386
  40.1 21.4 %all-to-all-done.refs_0_ = bf16[32,248,128]{2,1,0:T(8,128)(2,1)S(1)} async-done(((bf16[32,248,128]{2,1,0:T(8,128)(2,1)}), bf16[32,248,128]{2,1,0:T(8,128)(2,1)S(1)}, u32[]{:S(2)}, u32[]{:S(2)}) %all-to-all-start) | async-done | bytes 2031648 | tf_op jit(solution)/shard_map/all_to_all | solution.py:382
  61.6 3.4 %sweep.2 = (f32[8,152,128]{2,1,0:T(8,128)S(1)}, f32[8,152,128]{2,1,0:T(8,128)S(1)}, bf16[1280,768]{1,0:T(8,128)(2,1)S(1)}, f32[1,1280]{1,0:T(1,128)S(1)}) custom-call(s32[1]{0:T(128)} %bitcast.core, bf16[32,248,128]{2,1,0:T(8,128)(2,1)S(1)} %all-to-all-done.refs_0_, bf16[16,152,128]{2,1,0:T(8,128)(2,1)S(1)} %all_gather.6.refs_1_), custom_call_target="tpu_custom_call" | custom-call | tf_op jit(solution)/shard_map/sweep/pallas_call | solution.py:302
  65.0 4.5 %collective-permute-start = (f32[8,152,128]{2,1,0:T(8,128)S(1)}, f32[8,152,128]{2,1,0:T(8,128)S(1)}, u32[]{:S(2)}, u32[]{:S(2)}) collective-permute-start(f32[8,152,128]{2,1,0:T(8,128)S(1)} %get-tuple-element.16), channel_id=1, source_target_pairs={{0,1},{1,0},{2,3},{3,2},{4,5},{5,4},{6,7},{7,6},{8,9},{9,8},{10,11... | collective-permute-start | bytes 1867784 | tf_op jit(solution)/shard_map/ppermute | solution.py:389
  69.5 1.7 %collective-permute-done.received = f32[8,152,128]{2,1,0:T(8,128)S(1)} collective-permute-done((f32[8,152,128]{2,1,0:T(8,128)S(1)}, f32[8,152,128]{2,1,0:T(8,128)S(1)}, u32[]{:S(2)}, u32[]{:S(2)}) %collective-permute-start) | collective-permute-done | bytes 622624 | tf_op jit(solution)/shard_map/ppermute | solution.py:389
  71.1 0.1 join.2
  71.3 22.3 %all_to_all.15.parts = bf16[8,152,128]{2,1,0:T(8,128)(2,1)S(1)} all-to-all(bf16[8,152,128]{2,1,0:T(8,128)(2,1)S(1)} %join.2), channel_id=1, replica_groups={{0,2,4,6,8,10,12,14},{1,3,5,7,9,11,13,15},{16,18,20,22,24,26,28,30},{17..., dimensions={0} | all-to-all | bytes 622592 | tf_op jit(solution)/shard_map/all_to_all | solution.py:390
  93.5 0.1 update.2
  93.6 17.7 %all_gather.7.refs_2_ = bf16[16,152,128]{2,1,0:T(8,128)(2,1)S(1)} all-gather(bf16[1,152,128]{2,1,0:T(8,128)(2,1)S(1)} %get-tuple-element.17), channel_id=1, replica_groups=mesh['group'=32,'member'=16] {'member'}, dimensions={0}, use_global_device_ids=true | all-gather | bytes 661504 | tf_op jit(solution)/shard_map/all_gather | solution.py:386
  111.3 3.0 %sweep.3 = (f32[8,152,128]{2,1,0:T(8,128)S(1)}, f32[8,152,128]{2,1,0:T(8,128)S(1)}) custom-call(s32[1]{0:T(128)} %bitcast.core, bf16[1280,768]{1,0:T(8,128)(2,1)S(1)} %get-tuple-element.13.refs_0_, f32[1,1280]{1,0:T(1,128)S(1)} %get-tuple-element.14.refs_1_, bf16[16,152,128]{2,1,0:T(8,128)(2,1)S(1)} %all_gather.7.refs_2_), custom_call_target="tpu_custom_call" | custom-call | tf_op jit(solution)/shard_map/sweep/pallas_call | solution.py:302
  114.3 2.1 %collective-permute-start.1 = (f32[8,152,128]{2,1,0:T(8,128)S(1)}, f32[8,152,128]{2,1,0:T(8,128)S(1)}, u32[]{:S(2)}, u32[]{:S(2)}) collective-permute-start(f32[8,152,128]{2,1,0:T(8,128)S(1)} %get-tuple-element.19), channel_id=1, source_target_pairs={{0,1},{1,0},{2,3},{3,2},{4,5},{5,4},{6,7},{7,6},{8,9},{9,8},{10,11... | collective-permute-start | bytes 1867784 | tf_op jit(solution)/shard_map/ppermute | solution.py:389
  116.4 1.9 %collective-permute-done.1.received = f32[8,152,128]{2,1,0:T(8,128)S(1)} collective-permute-done((f32[8,152,128]{2,1,0:T(8,128)S(1)}, f32[8,152,128]{2,1,0:T(8,128)S(1)}, u32[]{:S(2)}, u32[]{:S(2)}) %collective-permute-start.1) | collective-permute-done | bytes 622624 | tf_op jit(solution)/shard_map/ppermute | solution.py:389
  118.3 0.1 join.3
  118.4 16.2 %all_to_all.16.parts = bf16[8,152,128]{2,1,0:T(8,128)(2,1)S(1)} all-to-all(bf16[8,152,128]{2,1,0:T(8,128)(2,1)S(1)} %join.3), channel_id=1, replica_groups={{0,2,4,6,8,10,12,14},{1,3,5,7,9,11,13,15},{16,18,20,22,24,26,28,30},{17..., dimensions={0} | all-to-all | bytes 622592 | tf_op jit(solution)/shard_map/all_to_all | solution.py:390
  134.6 0.7 update.3
  (1 shorter events, 0.0 us)
Async XLA Ops:
  3.8 10.7 %copy-start = (bf16[25,768]{1,0:T(8,128)(2,1)S(1)}, bf16[25,768]{1,0:T(8,128)(2,1)}, u32[]{:S(2)}) copy-start(bf16[25,768]{1,0:T(8,128)(2,1)} %prior.1) | copy-start | bytes 115204
  3.8 57.8 %all-to-all-start = ((bf16[32,248,128]{2,1,0:T(8,128)(2,1)}), bf16[32,248,128]{2,1,0:T(8,128)(2,1)S(1)}, u32[]{:S(2)}, u32[]{:S(2)}) async-start(bf16[32,248,128]{2,1,0:T(8,128)(2,1)} %front.1), calls=%async_computation | async-start | bytes 4063232 | tf_op jit(solution)/shard_map/all_to_all | solution.py:382
  65.0 6.2 %collective-permute-start = (f32[8,152,128]{2,1,0:T(8,128)S(1)}, f32[8,152,128]{2,1,0:T(8,128)S(1)}, u32[]{:S(2)}, u32[]{:S(2)}) collective-permute-start(f32[8,152,128]{2,1,0:T(8,128)S(1)} %get-tuple-element.16), channel_id=1, source_target_pairs={{0,1},{1,0},{2,3},{3,2},{4,5},{5,4},{6,7},{7,6},{8,9},{9,8},{10,11... | collective-permute-start | bytes 1867784 | tf_op jit(solution)/shard_map/ppermute | solution.py:389
  114.3 3.9 %collective-permute-start.1 = (f32[8,152,128]{2,1,0:T(8,128)S(1)}, f32[8,152,128]{2,1,0:T(8,128)S(1)}, u32[]{:S(2)}, u32[]{:S(2)}) collective-permute-start(f32[8,152,128]{2,1,0:T(8,128)S(1)} %get-tuple-element.19), channel_id=1, source_target_pairs={{0,1},{1,0},{2,3},{3,2},{4,5},{5,4},{6,7},{7,6},{8,9},{9,8},{10,11... | collective-permute-start | bytes 1867784 | tf_op jit(solution)/shard_map/ppermute | solution.py:389

commit v3 on v2

--- a/solution.py
+++ b/solution.py
@@ -26,7 +26,9 @@
 OWN = 25
 BLOCK = 32
 PACK = 152
-HALF = ZS * BLOCK
+MAIN = ZS * 24
+LASTS = 32
+PANEL = 2 * MAIN + LASTS
 ITEMS = GROUPS * CAP
 STEP = 256
 f32 = jnp.float32
@@ -216,34 +218,65 @@
     tags[...] = jnp.concatenate(pieces, axis=1) - 1.0
 
 
+def pack_sums(out, sums, lasts, totals, half):
+    which = iota((8, LANES), 0)
+    for z in range(ZS):
+        end = jnp.zeros((8, LANES), f32)
+        last = last_row(half, z)
+        for i in range(CHUNKS):
+            out[z, 24 * i : 24 * i + 24, :] = sums[24 * z : 24 * z + 24, chunk(i)]
+            end = jnp.where(which == i, lasts[last : last + 1, chunk(i)], end)
+        out[z, 144:, :] = jnp.where(which == 6, totals[z], end)
+
+
+def last_row(half, z):
+    return 8 * (z // 2) + 2 * half + z % 2
+
+
 def sweep_kernel(first, core, *refs):
     if first:
-        arrived, blocks, send, keep, items, tags, panel, weights, sums = refs
+        arrived, blocks, send, weights, marks, items, tags, panel, sums = refs
         unpack_items(arrived, items, tags)
     else:
-        items, tags, blocks, send, keep, panel, weights, sums = refs
+        items, tags, blocks, send, weights, marks, panel, sums = refs
 
     lengths = []
+    ends = []
     for half in range(2):
-        for z in range(ZS):
-            start = half * HALF + z * BLOCK
-            source = 2 * z + jnp.bitwise_xor(core[0], half)
-            end = blocks[source, 144:, :].astype(f32)
-            square = jnp.zeros((BLOCK, LANES), f32)
-            for q in range(CHUNKS // 2):
-                part = blocks[source, 48 * q : 48 * q + 48, :].astype(f32)
-                for i in (2 * q, 2 * q + 1):
-                    low = 24 * (i % 2)
-                    last = jnp.where(iota((8, LANES), 0) == 0, end[i : i + 1], 0.0)
-                    piece = jnp.concatenate([part[low : low + 24], last], axis=0)
-                    square = square + piece * piece
-                    panel[start : start + BLOCK, chunk(i)] = piece.astype(bf16)
-            lengths.append(jnp.sum(square, axis=1, keepdims=True))
+        for pair in range(ZS // 2):
+            squares = [jnp.zeros((24, LANES), f32) for _ in range(2)]
+            parts = []
+            for n in range(2):
+                source = 2 * (2 * pair + n) + jnp.bitwise_xor(core[0], half)
+                ends.append(blocks[source, 144:, :].astype(f32))
+                pieces = []
+                for q in range(CHUNKS // 2):
+                    part = blocks[source, 48 * q : 48 * q + 48, :].astype(f32)
+                    pieces += [part[:24], part[24:]]
+                for piece in pieces:
+                    squares[n] = squares[n] + piece * piece
+                parts.append(pieces)
+            start = half * MAIN + 48 * pair
+            for i in range(CHUNKS):
+                both = jnp.concatenate([parts[0][i], parts[1][i]], axis=0)
+                panel[start : start + 48, chunk(i)] = both.astype(bf16)
+            lengths += [jnp.sum(square, axis=1, keepdims=True) for square in squares]
+    square = jnp.zeros((LASTS, LANES), f32)
+    which = iota((LASTS, LANES), 0)
+    for i in range(CHUNKS):
+        piece = jnp.zeros((LASTS, LANES), f32)
+        for half in range(2):
+            for z in range(ZS):
+                row = ends[half * ZS + z][i : i + 1]
+                piece = jnp.where(which == last_row(half, z), row, piece)
+        square = square + piece * piece
+        panel[2 * MAIN :, chunk(i)] = piece.astype(bf16)
+    lengths.append(jnp.sum(square, axis=1, keepdims=True))
     lengths = jnp.concatenate(lengths, axis=0) * (1.0 / temper)
 
-    part_rows = HALF // CL_GRP
-    real = (iota((part_rows, 1), 0) % BLOCK) < OWN
-    totals = [jnp.zeros((part_rows, LANES), f32) for _ in range(2 * CL_GRP)]
+    starts = [(0, 48), (MAIN, 48), (2 * MAIN, 8)]
+    real = iota((8, 1), 0) < 4
+    totals = [[jnp.zeros((rows, LANES), f32) for _ in range(CL_GRP)] for _, rows in starts]
     for j in range(ITEMS // STEP):
         columns = slice(j * STEP, (j + 1) * STEP)
         product = lax.dot_general(
@@ -252,50 +285,47 @@
         logits = product * (2.0 / temper) - lengths
         tag = tags[:, columns]
         picked = []
-        for half in range(2):
-            rows = [
-                logits[half * HALF + c * part_rows : half * HALF + (c + 1) * part_rows]
-                for c in range(CL_GRP)
-            ]
-            chosen = rows[0]
+        for start, rows in starts:
+            chosen = logits[start : start + rows]
             for c in range(1, CL_GRP):
-                chosen = jnp.where(tag == c, rows[c], chosen)
-            picked.append(jnp.where(real, chosen, -3e38))
-        highest = jnp.maximum(
-            jnp.max(picked[0], axis=0, keepdims=True), jnp.max(picked[1], axis=0, keepdims=True)
-        )
+                chosen = jnp.where(tag == c, logits[start + c * rows : start + (c + 1) * rows], chosen)
+            picked.append(chosen)
+        picked[2] = jnp.where(real, picked[2], -3e38)
+        highest = functools.reduce(jnp.maximum, [jnp.max(p, axis=0, keepdims=True) for p in picked])
         exponent = [jnp.exp(p - highest) for p in picked]
-        scale = 1.0 / (
-            jnp.sum(exponent[0], axis=0, keepdims=True) + jnp.sum(exponent[1], axis=0, keepdims=True)
-        )
-        for half in range(2):
-            weight = exponent[half] * scale
+        scale = 1.0 / sum(jnp.sum(e, axis=0, keepdims=True) for e in exponent)
+        for n, (start, rows) in enumerate(starts):
+            weight = exponent[n] * scale
+            owned = [jnp.where(tag == c, weight, 0.0) for c in range(CL_GRP)]
             for c in range(CL_GRP):
-                own = jnp.where(tag == c, weight, 0.0)
-                start = half * HALF + c * part_rows
-                weights[start : start + part_rows, columns] = own.astype(bf16)
-                n = half * CL_GRP + c
                 for i in range(STEP // LANES):
-                    totals[n] = totals[n] + own[:, chunk(i)]
-
-    for half, out in ((1, send), (0, keep)):
-        sums[...] = jnp.dot(
-            weights[half * HALF : (half + 1) * HALF, :], items[...], preferred_element_type=f32
-        )
+                    totals[n][c] = totals[n][c] + owned[c][:, chunk(i)]
+            if rows % 16:
+                owned = [jnp.concatenate(owned[c : c + 2], axis=0) for c in range(0, CL_GRP, 2)]
+            for c, part in enumerate(owned):
+                size = part.shape[0]
+                weights[start + c * size : start + (c + 1) * size, columns] = part.astype(bf16)
+
+    lane = iota((1, LANES), 1)
+    rows_of = [[], []]
+    for half in range(2):
         for z in range(ZS):
-            start = z * BLOCK
-            end = jnp.zeros((8, LANES), f32)
-            for i in range(CHUNKS):
-                out[z, 24 * i : 24 * i + 24, :] = sums[start : start + 24, chunk(i)]
-                end = jnp.where(iota((8, LANES), 0) == i, sums[start + 24 : start + 25, chunk(i)], end)
-            block = totals[half * CL_GRP + z // 2][(z % 2) * BLOCK : (z % 2 + 1) * BLOCK]
-            total = to_row(jnp.sum(block, axis=1, keepdims=True))
-            out[z, 144:152, :] = jnp.where(iota((8, LANES), 0) == 6, total, end)
+            c, n = z // 2, z % 2
+            main = to_row(jnp.sum(totals[half][c][24 * n : 24 * n + 24], axis=1, keepdims=True))
+            last = jnp.sum(totals[2][c], axis=1, keepdims=True)[2 * half + n : 2 * half + n + 1]
+            rows_of[half].append(jnp.where(lane == 24, last, main))
+    for z in range(ZS):
+        marks[z, :, :] = jnp.broadcast_to(rows_of[0][z], (8, LANES))
+    sums[...] = jnp.dot(weights[MAIN:, :], items[...], preferred_element_type=f32)
+    pack_sums(send, sums, sums.at[MAIN:], rows_of[1], 1)
 
 
 def sweep(core, passages, blocks, first):
-    sums = jax.ShapeDtypeStruct((ZS, PACK, LANES), f32)
-    out_shape = [sums, sums]
+    out_shape = [
+        jax.ShapeDtypeStruct((ZS, PACK, LANES), f32),
+        jax.ShapeDtypeStruct((PANEL, ITEMS), bf16),
+        jax.ShapeDtypeStruct((ZS, 8, LANES), f32),
+    ]
     if first:
         out_shape.append(jax.ShapeDtypeStruct((ITEMS, CHUNKS * LANES), bf16))
         out_shape.append(jax.ShapeDtypeStruct((1, ITEMS), f32))
@@ -305,13 +335,34 @@
         in_specs=[SCALARS] + [ON_CHIP] * (len(passages) + 1),
         out_specs=[ON_CHIP] * len(out_shape),
         scratch_shapes=[
-            pltpu.VMEM((2 * HALF, CHUNKS * LANES), bf16),
-            pltpu.VMEM((2 * HALF, ITEMS), bf16),
-            pltpu.VMEM((HALF, CHUNKS * LANES), f32),
+            pltpu.VMEM((PANEL, CHUNKS * LANES), bf16),
+            pltpu.VMEM((MAIN + LASTS, CHUNKS * LANES), f32),
         ],
         compiler_params=pltpu.CompilerParams(vmem_limit_bytes=32 * 2**20),
         name="sweep",
     )(core, *passages, blocks)
+
+
+def kept_kernel(weights, items, marks, keep, sums, lasts):
+    sums[...] = jnp.dot(weights[:MAIN, :], items[...], preferred_element_type=f32)
+    lasts[...] = jnp.dot(weights[2 * MAIN :, :], items[...], preferred_element_type=f32)
+    pack_sums(keep, sums, lasts, [marks[z, :, :] for z in range(ZS)], 0)
+
+
+def kept(weights, items, marks):
+    features = CHUNKS * LANES
+    return pl.pallas_call(
+        kept_kernel,
+        out_shape=jax.ShapeDtypeStruct((ZS, PACK, LANES), f32),
+        in_specs=[ON_CHIP] * 3,
+        out_specs=ON_CHIP,
+        scratch_shapes=[pltpu.VMEM((MAIN, features), f32), pltpu.VMEM((LASTS, features), f32)],
+        cost_estimate=pl.CostEstimate(
+            flops=2 * (MAIN + LASTS) * ITEMS * features, bytes_accessed=4 * 2**20, transcendentals=0
+        ),
+        compiler_params=pltpu.CompilerParams(vmem_limit_bytes=16 * 2**20),
+        name="kept",
+    )(weights, items, marks)
 
 
 def join_kernel(keep, received, out):
@@ -384,9 +435,10 @@
     prior = centroids
     for turn in range(ITERS):
         blocks = lax.all_gather(packed, "member", axis=0, tiled=True)
-        send, keep, *unpacked = sweep(core, passage_refs, blocks, turn == 0)
+        send, weights, marks, *unpacked = sweep(core, passage_refs, blocks, turn == 0)
         passage_refs = unpacked or passage_refs
         received = lax.ppermute(send, "member", cores)
+        keep = kept(weights, passage_refs[0], marks)
         parts = lax.all_to_all(
             join(keep, received), "member", split_axis=0, concat_axis=0, tiled=True, axis_index_groups=along_z
         )

time: 136 us -> 133 us (0.978)
  waiting for transfers between devices: 25 us -> 23.3 us
    pallas_call x2, Pallas kernels: 6.42 us -> 4.11 us  [sweep(): pl.pallas_call(functools.partial(sweep_kernel, first), out_shape=out_shap...]
    ppermute x2, waiting for transfers between devices: 3.53 us -> 1.89 us  [shards(): received = lax.ppermute(send, 'member', cores)]
    pallas_call x0 -> x2, Pallas kernels: none -> 1.61 us  [kept(): pl.pallas_call(kept_kernel, out_shape=jax.ShapeDtypeStruct((ZS, PACK, LAN...]
  transfers between devices with their start and end apart: 3 -> 3, of which waited for: 3 -> 3; matrix products, arithmetic and copies ran while one was open for 0% -> 0% of each run, Pallas kernels for 0% -> 1%
where the time goes in v3:
time: 133 us
  blocking collectives  81.8 us (62%)
  waiting for transfers between devices  23.3 us (18%)
  starting transfers between devices  17.2 us (13%)
  Pallas kernels  10.5 us (8%)
    all_gather x2, blocking collectives, shards(): blocks = lax.all_gather(packed, 'member', axis=0, tiled=True)  43.3 us
    all_to_all x2, blocking collectives, shards(): lax.all_to_all(join(keep, received), 'member', split_axis=0, concat_axis=...  38.4 us
    all_to_all x1, waiting for transfers between devices, shards(): lax.all_to_all(outgoing, 'group', split_axis=0, concat_axis=0, tiled=True)  21.4 us
    all_to_all x1, starting transfers between devices, shards(): lax.all_to_all(outgoing, 'group', split_axis=0, concat_axis=0, tiled=True)  10.6 us
    ppermute x2, starting transfers between devices, shards(): received = lax.ppermute(send, 'member', cores)  6.59 us
    pallas_call x2, Pallas kernels, sweep(): pl.pallas_call(functools.partial(sweep_kernel, first), out_shape=out_shap...  4.11 us
    pallas_call x1, Pallas kernels, front(): pl.pallas_call(front_kernel, out_shape=jax.ShapeDtypeStruct(sent, bf16),...  3.75 us
  transfers between devices with their start and end apart: 3, of which 3 were waited for; matrix products, arithmetic and copies ran while one was open for 0% of the time, Pallas kernels for 1%

profile of v3, /device:TPU:1, one launch (start us, length us, event | category | flops | bytes accessed | tf_op | source)
XLA Modules:
  0.0 132.9 jit_solution(13889775561055487861)
XLA Ops:
  0.0 3.8 %front.1 = bf16[32,248,128]{2,1,0:T(8,128)(2,1)} custom-call(s32[1]{0:T(128)} %bitcast.1.me, s32[1,32]{1,0:T(1,128)} %counts_in.1, s32[1,32]{1,0:T(1,128)} %offsets_in.1, s32[8,128]{1,0:T(8,128)} %bitcast.4, s32[1,128]{1,0:T(1,128)} %bitcast.5, bf16[1024,768]{1,0:T(8,128)(2,1)} %rows_in.1), custom_call_target="tpu_custom_call" | custom-call | tf_op jit(solution)/shard_map/front/pallas_call | solution.py:136
  3.8 0.0 copy-start
  3.8 10.6 %all-to-all-start = ((bf16[32,248,128]{2,1,0:T(8,128)(2,1)}), bf16[32,248,128]{2,1,0:T(8,128)(2,1)S(1)}, u32[]{:S(2)}, u32[]{:S(2)}) async-start(bf16[32,248,128]{2,1,0:T(8,128)(2,1)} %front.1), calls=%async_computation | async-start | bytes 4063232 | tf_op jit(solution)/shard_map/all_to_all | solution.py:433
  14.4 0.0 copy-done
  14.5 25.7 %all_gather.6.refs_1_ = bf16[16,152,128]{2,1,0:T(8,128)(2,1)S(1)} all-gather(bf16[1,152,128]{2,1,0:T(8,128)(2,1)S(1)} %pack.1), channel_id=1, replica_groups=mesh['group'=32,'member'=16] {'member'}, dimensions={0}, use_global_device_ids=true | all-gather | bytes 661504 | tf_op jit(solution)/shard_map/all_gather | solution.py:437
  40.1 21.4 %all-to-all-done.refs_0_ = bf16[32,248,128]{2,1,0:T(8,128)(2,1)S(1)} async-done(((bf16[32,248,128]{2,1,0:T(8,128)(2,1)}), bf16[32,248,128]{2,1,0:T(8,128)(2,1)S(1)}, u32[]{:S(2)}, u32[]{:S(2)}) %all-to-all-start) | async-done | bytes 2031648 | tf_op jit(solution)/shard_map/all_to_all | solution.py:433
  61.6 2.3 %sweep.2 = (f32[8,152,128]{2,1,0:T(8,128)S(1)}, bf16[416,1280]{1,0:T(8,128)(2,1)S(1)}, f32[8,8,128]{2,1,0:T(8,128)S(1)}, bf16[1280,768]{1,0:T(8,128)(2,1)S(1)}, f32[1,1280]{1,0:T(1,128)S(1)}) custom-call(s32[1]{0:T(128)} %bitcast.core, bf16[32,248,128]{2,1,0:T(8,128)(2,1)S(1)} %all-to-all-done.refs_0_, bf16[16,152,128]{2,1,0:T(8,128)(2,1)S(1)} %all_gather.6.refs_1_), custom_call_target="tpu_custom_call" | custom-call | tf_op jit(solution)/shard_map/sweep/pallas_call | solution.py:332
  63.8 4.5 %collective-permute-start = (f32[8,152,128]{2,1,0:T(8,128)S(1)}, f32[8,152,128]{2,1,0:T(8,128)S(1)}, u32[]{:S(2)}, u32[]{:S(2)}) collective-permute-start(f32[8,152,128]{2,1,0:T(8,128)S(1)} %get-tuple-element.19), channel_id=1, source_target_pairs={{0,1},{1,0},{2,3},{3,2},{4,5},{5,4},{6,7},{7,6},{8,9},{9,8},{10,11... | collective-permute-start | bytes 1867784 | tf_op jit(solution)/shard_map/ppermute | solution.py:440
  68.3 0.8 kept.2.keep
  69.1 0.8 collective-permute-done.received
  70.0 0.1 join.2
  70.1 22.3 %all_to_all.15.parts = bf16[8,152,128]{2,1,0:T(8,128)(2,1)S(1)} all-to-all(bf16[8,152,128]{2,1,0:T(8,128)(2,1)S(1)} %join.2), channel_id=1, replica_groups={{0,2,4,6,8,10,12,14},{1,3,5,7,9,11,13,15},{16,18,20,22,24,26,28,30},{17..., dimensions={0} | all-to-all | bytes 622592 | tf_op jit(solution)/shard_map/all_to_all | solution.py:442
  92.3 0.1 update.2
  92.4 17.7 %all_gather.7.refs_2_ = bf16[16,152,128]{2,1,0:T(8,128)(2,1)S(1)} all-gather(bf16[1,152,128]{2,1,0:T(8,128)(2,1)S(1)} %get-tuple-element.20), channel_id=1, replica_groups=mesh['group'=32,'member'=16] {'member'}, dimensions={0}, use_global_device_ids=true | all-gather | bytes 661504 | tf_op jit(solution)/shard_map/all_gather | solution.py:437
  110.1 1.9 %sweep.3 = (f32[8,152,128]{2,1,0:T(8,128)S(1)}, bf16[416,1280]{1,0:T(8,128)(2,1)S(1)}, f32[8,8,128]{2,1,0:T(8,128)S(1)}) custom-call(s32[1]{0:T(128)} %bitcast.core, bf16[1280,768]{1,0:T(8,128)(2,1)S(1)} %get-tuple-element.15.items.refs_0_, f32[1,1280]{1,0:T(1,128)S(1)} %get-tuple-element.16.refs_1_, bf16[16,152,128]{2,1,0:T(8,128)(2,1)S(1)} %all_gather.7.refs_2_), custom_call_target="tpu_custom_call" | custom-call | tf_op jit(solution)/shard_map/sweep/pallas_call | solution.py:332
  112.0 2.1 %collective-permute-start.1 = (f32[8,152,128]{2,1,0:T(8,128)S(1)}, f32[8,152,128]{2,1,0:T(8,128)S(1)}, u32[]{:S(2)}, u32[]{:S(2)}) collective-permute-start(f32[8,152,128]{2,1,0:T(8,128)S(1)} %get-tuple-element.23), channel_id=1, source_target_pairs={{0,1},{1,0},{2,3},{3,2},{4,5},{5,4},{6,7},{7,6},{8,9},{9,8},{10,11... | collective-permute-start | bytes 1867784 | tf_op jit(solution)/shard_map/ppermute | solution.py:440
  114.1 0.8 kept.3.keep
  114.9 1.0 collective-permute-done.1.received
  115.9 0.1 join.3
  116.0 16.1 %all_to_all.16.parts = bf16[8,152,128]{2,1,0:T(8,128)(2,1)S(1)} all-to-all(bf16[8,152,128]{2,1,0:T(8,128)(2,1)S(1)} %join.3), channel_id=1, replica_groups={{0,2,4,6,8,10,12,14},{1,3,5,7,9,11,13,15},{16,18,20,22,24,26,28,30},{17..., dimensions={0} | all-to-all | bytes 622592 | tf_op jit(solution)/shard_map/all_to_all | solution.py:442
  132.1 0.7 update.3
  (1 shorter events, 0.0 us)
Async XLA Ops:
  3.8 10.7 %copy-start = (bf16[25,768]{1,0:T(8,128)(2,1)S(1)}, bf16[25,768]{1,0:T(8,128)(2,1)}, u32[]{:S(2)}) copy-start(bf16[25,768]{1,0:T(8,128)(2,1)} %prior.1) | copy-start | bytes 115204
  3.8 57.8 %all-to-all-start = ((bf16[32,248,128]{2,1,0:T(8,128)(2,1)}), bf16[32,248,128]{2,1,0:T(8,128)(2,1)S(1)}, u32[]{:S(2)}, u32[]{:S(2)}) async-start(bf16[32,248,128]{2,1,0:T(8,128)(2,1)} %front.1), calls=%async_computation | async-start | bytes 4063232 | tf_op jit(solution)/shard_map/all_to_all | solution.py:433
  63.8 6.2 %collective-permute-start = (f32[8,152,128]{2,1,0:T(8,128)S(1)}, f32[8,152,128]{2,1,0:T(8,128)S(1)}, u32[]{:S(2)}, u32[]{:S(2)}) collective-permute-start(f32[8,152,128]{2,1,0:T(8,128)S(1)} %get-tuple-element.19), channel_id=1, source_target_pairs={{0,1},{1,0},{2,3},{3,2},{4,5},{5,4},{6,7},{7,6},{8,9},{9,8},{10,11... | collective-permute-start | bytes 1867784 | tf_op jit(solution)/shard_map/ppermute | solution.py:440
  112.0 3.9 %collective-permute-start.1 = (f32[8,152,128]{2,1,0:T(8,128)S(1)}, f32[8,152,128]{2,1,0:T(8,128)S(1)}, u32[]{:S(2)}, u32[]{:S(2)}) collective-permute-start(f32[8,152,128]{2,1,0:T(8,128)S(1)} %get-tuple-element.23), channel_id=1, source_target_pairs={{0,1},{1,0},{2,3},{3,2},{4,5},{5,4},{6,7},{7,6},{8,9},{9,8},{10,11... | collective-permute-start | bytes 1867784 | tf_op jit(solution)/shard_map/ppermute | solution.py:440

commit v4 on v3

--- a/solution.py
+++ b/solution.py
@@ -21,7 +21,7 @@
 TAG_ROWS = 8
 SEND_ROWS = 240 + TAG_ROWS
 ROW_PARTS = 4
-OUT_PARTS = 4
+OUT_PARTS = 8
 ZS = 8
 OWN = 25
 BLOCK = 32
@@ -30,6 +30,7 @@
 LASTS = 32
 PANEL = 2 * MAIN + LASTS
 ITEMS = GROUPS * CAP
+HELD = ITEMS + 16
 STEP = 256
 f32 = jnp.float32
 bf16 = jnp.bfloat16
@@ -216,6 +217,13 @@
         tile = sum(tag_tile(16 * v + i) for i in range(16))
         pieces.append(tile[1:2])
     tags[...] = jnp.concatenate(pieces, axis=1) - 1.0
+    rows = [
+        jnp.concatenate([tags[:, start : start + ITEMS // 2], jnp.zeros((1, LANES), f32)], axis=1)
+        for start in (0, ITEMS // 2)
+    ]
+    which = iota((HELD - ITEMS, CHUNKS * LANES), 0)
+    held = jnp.where(which == 0, rows[0], jnp.where(which == 1, rows[1], 0.0))
+    items[ITEMS:, :] = held.astype(bf16)
 
 
 def pack_sums(out, sums, lasts, totals, half):
@@ -233,13 +241,8 @@
     return 8 * (z // 2) + 2 * half + z % 2
 
 
-def sweep_kernel(first, core, *refs):
-    if first:
-        arrived, blocks, send, weights, marks, items, tags, panel, sums = refs
-        unpack_items(arrived, items, tags)
-    else:
-        items, tags, blocks, send, weights, marks, panel, sums = refs
-
+def sweep_kernel(core, arrived, blocks, send, weights, marks, items, tags, panel, sums):
+    unpack_items(arrived, items, tags)
     lengths = []
     ends = []
     for half in range(2):
@@ -316,36 +319,35 @@
             rows_of[half].append(jnp.where(lane == 24, last, main))
     for z in range(ZS):
         marks[z, :, :] = jnp.broadcast_to(rows_of[0][z], (8, LANES))
-    sums[...] = jnp.dot(weights[MAIN:, :], items[...], preferred_element_type=f32)
+    sums[...] = jnp.dot(weights[MAIN:, :], items[:ITEMS, :], preferred_element_type=f32)
     pack_sums(send, sums, sums.at[MAIN:], rows_of[1], 1)
 
 
-def sweep(core, passages, blocks, first):
+def sweep(core, arrived, blocks):
     out_shape = [
         jax.ShapeDtypeStruct((ZS, PACK, LANES), f32),
         jax.ShapeDtypeStruct((PANEL, ITEMS), bf16),
         jax.ShapeDtypeStruct((ZS, 8, LANES), f32),
+        jax.ShapeDtypeStruct((HELD, CHUNKS * LANES), bf16),
     ]
-    if first:
-        out_shape.append(jax.ShapeDtypeStruct((ITEMS, CHUNKS * LANES), bf16))
-        out_shape.append(jax.ShapeDtypeStruct((1, ITEMS), f32))
-    return pl.pallas_call(
-        functools.partial(sweep_kernel, first),
+    return pl.pallas_call(
+        sweep_kernel,
         out_shape=out_shape,
-        in_specs=[SCALARS] + [ON_CHIP] * (len(passages) + 1),
+        in_specs=[SCALARS, ON_CHIP, ON_CHIP],
         out_specs=[ON_CHIP] * len(out_shape),
         scratch_shapes=[
+            pltpu.VMEM((1, ITEMS), f32),
             pltpu.VMEM((PANEL, CHUNKS * LANES), bf16),
             pltpu.VMEM((MAIN + LASTS, CHUNKS * LANES), f32),
         ],
         compiler_params=pltpu.CompilerParams(vmem_limit_bytes=32 * 2**20),
         name="sweep",
-    )(core, *passages, blocks)
+    )(core, arrived, blocks)
 
 
 def kept_kernel(weights, items, marks, keep, sums, lasts):
-    sums[...] = jnp.dot(weights[:MAIN, :], items[...], preferred_element_type=f32)
-    lasts[...] = jnp.dot(weights[2 * MAIN :, :], items[...], preferred_element_type=f32)
+    sums[...] = jnp.dot(weights[:MAIN, :], items[:ITEMS, :], preferred_element_type=f32)
+    lasts[...] = jnp.dot(weights[2 * MAIN :, :], items[:ITEMS, :], preferred_element_type=f32)
     pack_sums(keep, sums, lasts, [marks[z, :, :] for z in range(ZS)], 0)
 
 
@@ -365,14 +367,150 @@
     )(weights, items, marks)
 
 
+def held_tags(items):
+    rows = items[ITEMS:, :].astype(f32)
+    return jnp.concatenate([rows[n : n + 1, : ITEMS // 2] for n in range(2)], axis=1)
+
+
+def half_kernel(items, others, mine, exponents, stats, panel):
+    lengths = []
+    ends = []
+    for pair in range(ZS // 2):
+        squares = [jnp.zeros((24, LANES), f32) for _ in range(2)]
+        parts = []
+        for n in range(2):
+            z = 2 * pair + n
+            ends.append(mine[z, 144:, :].astype(f32))
+            pieces = []
+            for q in range(CHUNKS // 2):
+                part = mine[z, 48 * q : 48 * q + 48, :].astype(f32)
+                pieces += [part[:24], part[24:]]
+            for piece in pieces:
+                squares[n] = squares[n] + piece * piece
+            parts.append(pieces)
+        for i in range(CHUNKS):
+            both = jnp.concatenate([parts[0][i], parts[1][i]], axis=0)
+            panel[48 * pair : 48 * pair + 48, chunk(i)] = both.astype(bf16)
+        lengths += [jnp.sum(square, axis=1, keepdims=True) for square in squares]
+    square = jnp.zeros((LASTS, LANES), f32)
+    which = iota((LASTS, LANES), 0)
+    for i in range(CHUNKS):
+        piece = jnp.zeros((LASTS, LANES), f32)
+        for z in range(ZS):
+            piece = jnp.where(which == last_row(0, z), ends[z][i : i + 1], piece)
+        square = square + piece * piece
+        panel[MAIN:, chunk(i)] = piece.astype(bf16)
+    lengths.append(jnp.sum(square, axis=1, keepdims=True))
+    lengths = jnp.concatenate(lengths, axis=0) * (1.0 / temper)
+
+    real = iota((8, 1), 0) < 2
+    for side, source in enumerate((items, others)):
+        tags = held_tags(source)
+        for j in range(ITEMS // STEP):
+            columns = slice(j * STEP, (j + 1) * STEP)
+            product = lax.dot_general(
+                panel[...], source[columns, :], (((1,), (1,)), ((), ())), preferred_element_type=f32
+            )
+            logits = product * (2.0 / temper) - lengths
+            tag = tags[:, columns]
+            picked = []
+            for start, rows in ((0, 48), (MAIN, 8)):
+                chosen = logits[start : start + rows]
+                for c in range(1, CL_GRP):
+                    chosen = jnp.where(tag == c, logits[start + c * rows : start + (c + 1) * rows], chosen)
+                picked.append(chosen)
+            picked[1] = jnp.where(real, picked[1], -3e38)
+            highest = jnp.maximum(
+                jnp.max(picked[0], axis=0, keepdims=True), jnp.max(picked[1], axis=0, keepdims=True)
+            )
+            main, last = [jnp.exp(p - highest) for p in picked]
+            place = slice(side * ITEMS + j * STEP, side * ITEMS + (j + 1) * STEP)
+            exponents[:48, place] = main
+            exponents[48:, place] = last
+            total = jnp.sum(main, axis=0, keepdims=True) + jnp.sum(last, axis=0, keepdims=True)
+            stats[:, place] = jnp.where(iota((8, STEP), 0) == 0, highest, total)
+
+
+def half_logits(items, others, mine):
+    return pl.pallas_call(
+        half_kernel,
+        out_shape=[jax.ShapeDtypeStruct((56, 2 * ITEMS), f32), jax.ShapeDtypeStruct((8, 2 * ITEMS), f32)],
+        in_specs=[ON_CHIP] * 3,
+        out_specs=[ON_CHIP] * 2,
+        scratch_shapes=[pltpu.VMEM((MAIN + LASTS, CHUNKS * LANES), bf16)],
+        compiler_params=pltpu.CompilerParams(vmem_limit_bytes=32 * 2**20),
+        name="half_logits",
+    )(items, others, mine)
+
+
+def half_sums_kernel(exponents, stats, theirs, items, others, out, weights, sums):
+    totals = [jnp.zeros((48, LANES), f32) for _ in range(CL_GRP)]
+    last_totals = [jnp.zeros((8, LANES), f32) for _ in range(CL_GRP)]
+    for side, source in enumerate((items, others)):
+        tags = held_tags(source)
+        for j in range(ITEMS // STEP):
+            tag = tags[:, j * STEP : (j + 1) * STEP]
+            place = slice(side * ITEMS + j * STEP, side * ITEMS + (j + 1) * STEP)
+            there = slice((1 - side) * ITEMS + j * STEP, (1 - side) * ITEMS + (j + 1) * STEP)
+            top, other_top = stats[0:1, place], theirs[0:1, there]
+            highest = jnp.maximum(top, other_top)
+            share = jnp.exp(top - highest)
+            whole = stats[1:2, place] * share + theirs[1:2, there] * jnp.exp(other_top - highest)
+            scale = share / whole
+            weight = exponents[:, place] * scale
+            owned = [jnp.where(tag == c, weight, 0.0) for c in range(CL_GRP)]
+            for c in range(CL_GRP):
+                for i in range(STEP // LANES):
+                    totals[c] = totals[c] + owned[c][:48, chunk(i)]
+                    last_totals[c] = last_totals[c] + owned[c][48:, chunk(i)]
+                weights[48 * c : 48 * c + 48, place] = owned[c][:48].astype(bf16)
+            for c in range(0, CL_GRP, 2):
+                both = jnp.concatenate([owned[c][48:], owned[c + 1][48:]], axis=0)
+                weights[MAIN + 8 * c : MAIN + 8 * c + 16, place] = both.astype(bf16)
+    sums[...] = jnp.dot(weights[:, :ITEMS], items[:ITEMS, :], preferred_element_type=f32) + jnp.dot(
+        weights[:, ITEMS:], others[:ITEMS, :], preferred_element_type=f32
+    )
+    which = iota((8, LANES), 0)
+    lane = iota((1, LANES), 1)
+    for z in range(ZS):
+        c, n = z // 2, z % 2
+        row = MAIN + last_row(0, z)
+        end = jnp.zeros((8, LANES), f32)
+        for i in range(CHUNKS):
+            end = jnp.where(which == i, sums[row : row + 1, chunk(i)], end)
+        main = to_row(jnp.sum(totals[c][24 * n : 24 * n + 24], axis=1, keepdims=True))
+        last = jnp.sum(last_totals[c], axis=1, keepdims=True)[n : n + 1]
+        end = jnp.where(which == 6, jnp.where(lane == 24, last, main), end)
+        for q in range(CHUNKS // 2):
+            both = [sums[24 * z : 24 * z + 24, chunk(i)] for i in (2 * q, 2 * q + 1)]
+            out[z, 48 * q : 48 * q + 48, :] = jnp.concatenate(both, axis=0).astype(bf16)
+        out[z, 144:, :] = with_rest(end).astype(bf16)
+
+
+def half_sums(exponents, stats, theirs, items, others):
+    return pl.pallas_call(
+        half_sums_kernel,
+        out_shape=jax.ShapeDtypeStruct((ZS, PACK, LANES), bf16),
+        in_specs=[ON_CHIP] * 5,
+        out_specs=ON_CHIP,
+        scratch_shapes=[
+            pltpu.VMEM((MAIN + LASTS, 2 * ITEMS), bf16),
+            pltpu.VMEM((MAIN + LASTS, CHUNKS * LANES), f32),
+        ],
+        compiler_params=pltpu.CompilerParams(vmem_limit_bytes=32 * 2**20),
+        name="half_sums",
+    )(exponents, stats, theirs, items, others)
+
+
+def with_rest(end):
+    rest = end - end.astype(bf16).astype(f32)
+    return jnp.where(iota((8, LANES), 0) == 7, rest[6:7], end)
+
+
 def join_kernel(keep, received, out):
-    which = iota((8, LANES), 0)
     for z in range(ZS):
         out[z, :144, :] = (keep[z, :144, :] + received[z, :144, :]).astype(bf16)
-        end = keep[z, 144:152, :] + received[z, 144:152, :]
-        rest = end - end.astype(bf16).astype(f32)
-        end = jnp.where(which == 7, rest[6:7], end)
-        out[z, 144:, :] = end.astype(bf16)
+        out[z, 144:, :] = with_rest(keep[z, 144:, :] + received[z, 144:, :]).astype(bf16)
 
 
 def join(keep, received):
@@ -386,7 +524,7 @@
     )(keep, received)
 
 
-def update_kernel(parts, prior, out, *packed):
+def update_kernel(parts, prior, out, *copies):
     total = parts[0].astype(f32)
     for z in range(1, ZS):
         total = total + parts[z].astype(f32)
@@ -401,17 +539,20 @@
         out[24:25, chunk(i)] = last
         pieces.append(piece)
         lasts.append(last)
-    if packed:
+    if copies:
         parts, end = pack_rows(pieces, lasts)
-        for q in range(CHUNKS // 2):
-            packed[0][0, 48 * q : 48 * q + 48, :] = parts[q].astype(bf16)
-        packed[0][0, 144:, :] = end.astype(bf16)
+        parts = [part.astype(bf16) for part in parts]
+        end = end.astype(bf16)
+        for z in range(ZS):
+            for q in range(CHUNKS // 2):
+                copies[0][z, 48 * q : 48 * q + 48, :] = parts[q]
+            copies[0][z, 144:, :] = end
 
 
 def update(parts, prior, last):
     out_shape = [jax.ShapeDtypeStruct((OWN, CHUNKS * LANES), f32)]
     if not last:
-        out_shape.append(jax.ShapeDtypeStruct((1, PACK, LANES), bf16))
+        out_shape.append(jax.ShapeDtypeStruct((ZS, PACK, LANES), bf16))
     return pl.pallas_call(
         update_kernel,
         out_shape=out_shape,
@@ -429,22 +570,24 @@
     me = lax.axis_index("group").reshape(1).astype(jnp.int32)
     core = jnp.bitwise_and(lax.axis_index("member"), 1).reshape(1).astype(jnp.int32)
 
+    def along(blocks):
+        return lax.all_to_all(
+            blocks, "member", split_axis=0, concat_axis=0, tiled=True, axis_index_groups=along_z
+        )
+
     outgoing = front(me, send_counts, send_offsets, labels, owner_slot, passages)
-    passage_refs = [lax.all_to_all(outgoing, "group", split_axis=0, concat_axis=0, tiled=True)]
-    packed = pack(centroids)
-    prior = centroids
-    for turn in range(ITERS):
-        blocks = lax.all_gather(packed, "member", axis=0, tiled=True)
-        send, weights, marks, *unpacked = sweep(core, passage_refs, blocks, turn == 0)
-        passage_refs = unpacked or passage_refs
-        received = lax.ppermute(send, "member", cores)
-        keep = kept(weights, passage_refs[0], marks)
-        parts = lax.all_to_all(
-            join(keep, received), "member", split_axis=0, concat_axis=0, tiled=True, axis_index_groups=along_z
-        )
-        prior, *packed = update(parts, prior, turn == ITERS - 1)
-        packed = packed[0] if packed else None
-    return prior
+    arrived = lax.all_to_all(outgoing, "group", split_axis=0, concat_axis=0, tiled=True)
+    blocks = lax.all_gather(pack(centroids), "member", axis=0, tiled=True)
+    send, weights, marks, items = sweep(core, arrived, blocks)
+    received = lax.ppermute(send, "member", cores)
+    joined = join(kept(weights, items, marks), received)
+    items, joined = lax.optimization_barrier((items, joined))
+    others = lax.ppermute(items, "member", cores)
+    current, copies = update(along(joined), centroids, False)
+    exponents, stats = half_logits(items, others, along(copies))
+    theirs = lax.ppermute(stats, "member", cores)
+    (current,) = update(along(half_sums(exponents, stats, theirs, items, others)), current, True)
+    return current
 
 
 def solution(mesh):

time: 133 us -> 133 us (level)
  starting transfers between devices: 17.2 us -> 22.3 us
  blocking collectives: 81.8 us -> 77 us
    all_gather x2 -> x1, blocking collectives: 43.3 us -> 25.7 us  [shards(): blocks = lax.all_gather(pack(centroids), 'member', axis=0, tiled=True)]
    all_to_all x2 -> x3, blocking collectives: 38.4 us -> 51.3 us  [along(): lax.all_to_all(blocks, 'member', split_axis=0, concat_axis=0, tiled=True,...]
    ppermute x0 -> x2, starting transfers between devices: none -> 7.15 us  [the longest x1 4.86 us: shards(): theirs = lax.ppermute(stats, 'member', cores)]
    ppermute x2 -> x1, starting transfers between devices: 6.59 us -> 4.52 us  [shards(): received = lax.ppermute(send, 'member', cores)]
    pallas_call x2 -> x3, Pallas kernels: 4.11 us -> 4.81 us  [the longest x1 2.25 us: sweep(): pl.pallas_call(sweep_kernel, out_shape=out_shape, in_specs=[SCALARS, ON_C...]
  transfers between devices with their start and end apart: 3 -> 4, of which waited for: 3 -> 3; matrix products, arithmetic and copies ran while one was open for 0% -> 0% of each run, Pallas kernels for 1% -> 1%
where the time goes in v4:
time: 133 us
  blocking collectives  77 us (58%)
  waiting for transfers between devices  23.2 us (17%)
  starting transfers between devices  22.3 us (17%)
  Pallas kernels  10.1 us (8%)
    all_to_all x3, blocking collectives, along(): lax.all_to_all(blocks, 'member', split_axis=0, concat_axis=0, tiled=True,...  51.3 us
    all_gather x1, blocking collectives, shards(): blocks = lax.all_gather(pack(centroids), 'member', axis=0, tiled=True)  25.7 us
    all_to_all x1, waiting for transfers between devices, shards(): lax.all_to_all(outgoing, 'group', split_axis=0, concat_axis=0, tiled=True)  21.4 us
    all_to_all x1, starting transfers between devices, shards(): lax.all_to_all(outgoing, 'group', split_axis=0, concat_axis=0, tiled=True)  10.6 us
    ppermute x1, starting transfers between devices, shards(): theirs = lax.ppermute(stats, 'member', cores)  4.86 us
    ppermute x1, starting transfers between devices, shards(): received = lax.ppermute(send, 'member', cores)  4.52 us
    pallas_call x1, Pallas kernels, front(): pl.pallas_call(front_kernel, out_shape=jax.ShapeDtypeStruct(sent, bf16),...  3.57 us
  transfers between devices with their start and end apart: 4, of which 3 were waited for; matrix products, arithmetic and copies ran while one was open for 0% of the time, Pallas kernels for 1%

profile of v4, /device:TPU:1, one launch (start us, length us, event | category | flops | bytes accessed | tf_op | source)
XLA Modules:
  0.0 132.7 jit_solution(3789917199743628017)
XLA Ops:
  0.0 3.6 %front.1 = bf16[32,248,128]{2,1,0:T(8,128)(2,1)} custom-call(s32[1]{0:T(128)} %bitcast.1.me, s32[1,32]{1,0:T(1,128)} %counts_in.1, s32[1,32]{1,0:T(1,128)} %offsets_in.1, s32[8,128]{1,0:T(8,128)} %bitcast.4, s32[1,128]{1,0:T(1,128)} %bitcast.5, bf16[1024,768]{1,0:T(8,128)(2,1)} %rows_in.1), custom_call_target="tpu_custom_call" | custom-call | tf_op jit(solution)/shard_map/front/pallas_call | solution.py:137
  3.6 0.0 copy-start
  3.6 10.6 %all-to-all-start = ((bf16[32,248,128]{2,1,0:T(8,128)(2,1)}), bf16[32,248,128]{2,1,0:T(8,128)(2,1)S(1)}, u32[]{:S(2)}, u32[]{:S(2)}) async-start(bf16[32,248,128]{2,1,0:T(8,128)(2,1)} %front.1), calls=%async_computation | async-start | bytes 4063232 | tf_op jit(solution)/shard_map/all_to_all | solution.py:579
  14.2 0.0 copy-done
  14.3 25.7 %all_gather.3.blocks = bf16[16,152,128]{2,1,0:T(8,128)(2,1)S(1)} all-gather(bf16[1,152,128]{2,1,0:T(8,128)(2,1)S(1)} %pack.1), channel_id=1, replica_groups=mesh['group'=32,'member'=16] {'member'}, dimensions={0}, use_global_device_ids=true | all-gather | bytes 661504 | tf_op jit(solution)/shard_map/all_gather | solution.py:580
  39.9 21.4 %all-to-all-done.arrived = bf16[32,248,128]{2,1,0:T(8,128)(2,1)S(1)} async-done(((bf16[32,248,128]{2,1,0:T(8,128)(2,1)}), bf16[32,248,128]{2,1,0:T(8,128)(2,1)S(1)}, u32[]{:S(2)}, u32[]{:S(2)}) %all-to-all-start) | async-done | bytes 2031648 | tf_op jit(solution)/shard_map/all_to_all | solution.py:579
  61.4 2.3 %sweep.1 = (f32[8,152,128]{2,1,0:T(8,128)S(1)}, bf16[416,1280]{1,0:T(8,128)(2,1)S(1)}, f32[8,8,128]{2,1,0:T(8,128)S(1)}, bf16[1296,768]{1,0:T(8,128)(2,1)S(1)}) custom-call(s32[1]{0:T(128)} %bitcast.core, bf16[32,248,128]{2,1,0:T(8,128)(2,1)S(1)} %all-to-all-done.arrived, bf16[16,152,128]{2,1,0:T(8,128)(2,1)S(1)} %all_gather.3.blocks), custom_call_target="tpu_custom_call" | custom-call | tf_op jit(solution)/shard_map/sweep/pallas_call | solution.py:333
  63.6 4.5 %collective-permute-start = (f32[8,152,128]{2,1,0:T(8,128)S(1)}, f32[8,152,128]{2,1,0:T(8,128)S(1)}, u32[]{:S(2)}, u32[]{:S(2)}) collective-permute-start(f32[8,152,128]{2,1,0:T(8,128)S(1)} %get-tuple-element.18), channel_id=1, source_target_pairs={{0,1},{1,0},{2,3},{3,2},{4,5},{5,4},{6,7},{7,6},{8,9},{9,8},{10,11... | collective-permute-start | bytes 1867784 | tf_op jit(solution)/shard_map/ppermute | solution.py:582
  68.2 0.8 kept.1.keep
  69.0 0.8 collective-permute-done.received
  69.8 0.1 join.1
  69.9 2.3 %collective-permute-start.1 = (bf16[1296,768]{1,0:T(8,128)(2,1)S(1)}, bf16[1296,768]{1,0:T(8,128)(2,1)S(1)}, u32[]{:S(2)}, u32[]{:S(2)}) collective-permute-start(bf16[1296,768]{1,0:T(8,128)(2,1)S(1)} %get-tuple-element.19.items), channel_id=1, source_target_pairs={{0,1},{1,0},{2,3},{3,2},{4,5},{5,4},{6,7},{7,6},{8,9},{9,8},{10,11... | collective-permute-start | bytes 5971976 | tf_op jit(solution)/shard_map/ppermute | solution.py:585
  72.2 22.7 %all_to_all.20.parts = bf16[8,152,128]{2,1,0:T(8,128)(2,1)S(1)} all-to-all(bf16[8,152,128]{2,1,0:T(8,128)(2,1)S(1)} %join.1), channel_id=1, replica_groups={{0,2,4,6,8,10,12,14},{1,3,5,7,9,11,13,15},{16,18,20,22,24,26,28,30},{17..., dimensions={0} | all-to-all | bytes 622592 | tf_op jit(solution)/shard_map/all_to_all | solution.py:574
  94.8 0.1 update.2
  95.0 13.3 %all_to_all.21.mine = bf16[8,152,128]{2,1,0:T(8,128)(2,1)S(1)} all-to-all(bf16[8,152,128]{2,1,0:T(8,128)(2,1)S(1)} %get-tuple-element.21), channel_id=1, replica_groups={{0,2,4,6,8,10,12,14},{1,3,5,7,9,11,13,15},{16,18,20,22,24,26,28,30},{17..., dimensions={0} | all-to-all | bytes 622592 | tf_op jit(solution)/shard_map/all_to_all | solution.py:574
  108.3 0.0 collective-permute-done.1.others
  108.3 1.4 %half_logits.1 = (f32[56,2560]{1,0:T(8,128)S(1)}, f32[8,2560]{1,0:T(8,128)S(1)}) custom-call(bf16[1296,768]{1,0:T(8,128)(2,1)S(1)} %get-tuple-element.19.items, bf16[1296,768]{1,0:T(8,128)(2,1)S(1)} %collective-permute-done.1.others, bf16[8,152,128]{2,1,0:T(8,128)(2,1)S(1)} %all_to_all.21.mine), custom_call_target="tpu_custom_call" | custom-call | tf_op jit(solution)/shard_map/half_logits/pallas_call | solution.py:435
  109.7 4.9 %collective-permute-start.2 = (f32[8,2560]{1,0:T(8,128)S(1)}, f32[8,2560]{1,0:T(8,128)S(1)}, u32[]{:S(2)}, u32[]{:S(2)}) collective-permute-start(f32[8,2560]{1,0:T(8,128)S(1)} %get-tuple-element.23.stats), channel_id=1, source_target_pairs={{0,1},{1,0},{2,3},{3,2},{4,5},{5,4},{6,7},{7,6},{8,9},{9,8},{10,11... | collective-permute-start | bytes 245768 | tf_op jit(solution)/shard_map/ppermute | solution.py:588
  114.6 0.9 collective-permute-done.2.theirs
  115.5 1.1 half_sums.1
  116.6 15.4 %all_to_all.22.parts = bf16[8,152,128]{2,1,0:T(8,128)(2,1)S(1)} all-to-all(bf16[8,152,128]{2,1,0:T(8,128)(2,1)S(1)} %half_sums.1), channel_id=1, replica_groups={{0,2,4,6,8,10,12,14},{1,3,5,7,9,11,13,15},{16,18,20,22,24,26,28,30},{17..., dimensions={0} | all-to-all | bytes 622592 | tf_op jit(solution)/shard_map/all_to_all | solution.py:574
  132.0 0.7 update.3
  (1 shorter events, 0.0 us)
Async XLA Ops:
  3.6 10.7 %copy-start = (bf16[25,768]{1,0:T(8,128)(2,1)S(1)}, bf16[25,768]{1,0:T(8,128)(2,1)}, u32[]{:S(2)}) copy-start(bf16[25,768]{1,0:T(8,128)(2,1)} %prior.1) | copy-start | bytes 115204
  3.6 57.8 %all-to-all-start = ((bf16[32,248,128]{2,1,0:T(8,128)(2,1)}), bf16[32,248,128]{2,1,0:T(8,128)(2,1)S(1)}, u32[]{:S(2)}, u32[]{:S(2)}) async-start(bf16[32,248,128]{2,1,0:T(8,128)(2,1)} %front.1), calls=%async_computation | async-start | bytes 4063232 | tf_op jit(solution)/shard_map/all_to_all | solution.py:579
  63.6 6.2 %collective-permute-start = (f32[8,152,128]{2,1,0:T(8,128)S(1)}, f32[8,152,128]{2,1,0:T(8,128)S(1)}, u32[]{:S(2)}, u32[]{:S(2)}) collective-permute-start(f32[8,152,128]{2,1,0:T(8,128)S(1)} %get-tuple-element.18), channel_id=1, source_target_pairs={{0,1},{1,0},{2,3},{3,2},{4,5},{5,4},{6,7},{7,6},{8,9},{9,8},{10,11... | collective-permute-start | bytes 1867784 | tf_op jit(solution)/shard_map/ppermute | solution.py:582
  69.9 38.4 %collective-permute-start.1 = (bf16[1296,768]{1,0:T(8,128)(2,1)S(1)}, bf16[1296,768]{1,0:T(8,128)(2,1)S(1)}, u32[]{:S(2)}, u32[]{:S(2)}) collective-permute-start(bf16[1296,768]{1,0:T(8,128)(2,1)S(1)} %get-tuple-element.19.items), channel_id=1, source_target_pairs={{0,1},{1,0},{2,3},{3,2},{4,5},{5,4},{6,7},{7,6},{8,9},{9,8},{10,11... | collective-permute-start | bytes 5971976 | tf_op jit(solution)/shard_map/ppermute | solution.py:585
  109.7 5.8 %collective-permute-start.2 = (f32[8,2560]{1,0:T(8,128)S(1)}, f32[8,2560]{1,0:T(8,128)S(1)}, u32[]{:S(2)}, u32[]{:S(2)}) collective-permute-start(f32[8,2560]{1,0:T(8,128)S(1)} %get-tuple-element.23.stats), channel_id=1, source_target_pairs={{0,1},{1,0},{2,3},{3,2},{4,5},{5,4},{6,7},{7,6},{8,9},{9,8},{10,11... | collective-permute-start | bytes 245768 | tf_op jit(solution)/shard_map/ppermute | solution.py:588

commit v5 on v3

--- a/solution.py
+++ b/solution.py
@@ -21,7 +21,7 @@
 TAG_ROWS = 8
 SEND_ROWS = 240 + TAG_ROWS
 ROW_PARTS = 4
-OUT_PARTS = 4
+OUT_PARTS = 8
 ZS = 8
 OWN = 25
 BLOCK = 32
@@ -233,6 +233,16 @@
     return 8 * (z // 2) + 2 * half + z % 2
 
 
+def total_rows(main, last, half):
+    rows = []
+    for z in range(ZS):
+        c, n = z // 2, z % 2
+        row = to_row(jnp.sum(main[c][24 * n : 24 * n + 24], axis=1, keepdims=True))
+        end = jnp.sum(last[c], axis=1, keepdims=True)[2 * half + n : 2 * half + n + 1]
+        rows.append(jnp.where(iota((1, LANES), 1) == 24, end, row))
+    return rows
+
+
 def sweep_kernel(first, core, *refs):
     if first:
         arrived, blocks, send, weights, marks, items, tags, panel, sums = refs
@@ -306,25 +316,18 @@
                 size = part.shape[0]
                 weights[start + c * size : start + (c + 1) * size, columns] = part.astype(bf16)
 
-    lane = iota((1, LANES), 1)
-    rows_of = [[], []]
-    for half in range(2):
-        for z in range(ZS):
-            c, n = z // 2, z % 2
-            main = to_row(jnp.sum(totals[half][c][24 * n : 24 * n + 24], axis=1, keepdims=True))
-            last = jnp.sum(totals[2][c], axis=1, keepdims=True)[2 * half + n : 2 * half + n + 1]
-            rows_of[half].append(jnp.where(lane == 24, last, main))
-    for z in range(ZS):
-        marks[z, :, :] = jnp.broadcast_to(rows_of[0][z], (8, LANES))
+    for c in range(CL_GRP):
+        marks[c, :48, :] = totals[0][c]
+        marks[c, 48:, :] = totals[2][c]
     sums[...] = jnp.dot(weights[MAIN:, :], items[...], preferred_element_type=f32)
-    pack_sums(send, sums, sums.at[MAIN:], rows_of[1], 1)
+    pack_sums(send, sums, sums.at[MAIN:], total_rows(totals[1], totals[2], 1), 1)
 
 
 def sweep(core, passages, blocks, first):
     out_shape = [
         jax.ShapeDtypeStruct((ZS, PACK, LANES), f32),
         jax.ShapeDtypeStruct((PANEL, ITEMS), bf16),
-        jax.ShapeDtypeStruct((ZS, 8, LANES), f32),
+        jax.ShapeDtypeStruct((CL_GRP, 56, LANES), f32),
     ]
     if first:
         out_shape.append(jax.ShapeDtypeStruct((ITEMS, CHUNKS * LANES), bf16))
@@ -346,7 +349,9 @@
 def kept_kernel(weights, items, marks, keep, sums, lasts):
     sums[...] = jnp.dot(weights[:MAIN, :], items[...], preferred_element_type=f32)
     lasts[...] = jnp.dot(weights[2 * MAIN :, :], items[...], preferred_element_type=f32)
-    pack_sums(keep, sums, lasts, [marks[z, :, :] for z in range(ZS)], 0)
+    main = [marks[c, :48, :] for c in range(CL_GRP)]
+    last = [marks[c, 48:, :] for c in range(CL_GRP)]
+    pack_sums(keep, sums, lasts, total_rows(main, last, 0), 0)
 
 
 def kept(weights, items, marks):

time: 133 us -> 133 us (level)
  no operation moved by 1% of the time
where the time goes in v5:
time: 133 us
  blocking collectives  81.8 us (62%)
  waiting for transfers between devices  23.3 us (18%)
  starting transfers between devices  17.2 us (13%)
  Pallas kernels  10.5 us (8%)
    all_gather x2, blocking collectives, shards(): blocks = lax.all_gather(packed, 'member', axis=0, tiled=True)  43.3 us
    all_to_all x2, blocking collectives, shards(): lax.all_to_all(join(keep, received), 'member', split_axis=0, concat_axis=...  38.4 us
    all_to_all x1, waiting for transfers between devices, shards(): lax.all_to_all(outgoing, 'group', split_axis=0, concat_axis=0, tiled=True)  21.4 us
    all_to_all x1, starting transfers between devices, shards(): lax.all_to_all(outgoing, 'group', split_axis=0, concat_axis=0, tiled=True)  10.6 us
    ppermute x2, starting transfers between devices, shards(): received = lax.ppermute(send, 'member', cores)  6.58 us
    pallas_call x2, Pallas kernels, sweep(): pl.pallas_call(functools.partial(sweep_kernel, first), out_shape=out_shap...  4.29 us
    pallas_call x1, Pallas kernels, front(): pl.pallas_call(front_kernel, out_shape=jax.ShapeDtypeStruct(sent, bf16),...  3.58 us
  transfers between devices with their start and end apart: 3, of which 3 were waited for; matrix products, arithmetic and copies ran while one was open for 0% of the time, Pallas kernels for 1%

profile of v5, /device:TPU:1, one launch (start us, length us, event | category | flops | bytes accessed | tf_op | source)
XLA Modules:
  0.0 132.9 jit_solution(2955137904712688019)
XLA Ops:
  0.0 3.6 %front.1 = bf16[32,248,128]{2,1,0:T(8,128)(2,1)} custom-call(s32[1]{0:T(128)} %bitcast.1.me, s32[1,32]{1,0:T(1,128)} %counts_in.1, s32[1,32]{1,0:T(1,128)} %offsets_in.1, s32[8,128]{1,0:T(8,128)} %bitcast.4, s32[1,128]{1,0:T(1,128)} %bitcast.5, bf16[1024,768]{1,0:T(8,128)(2,1)} %rows_in.1), custom_call_target="tpu_custom_call" | custom-call | tf_op jit(solution)/shard_map/front/pallas_call | solution.py:136
  3.6 0.0 copy-start
  3.6 10.6 %all-to-all-start = ((bf16[32,248,128]{2,1,0:T(8,128)(2,1)}), bf16[32,248,128]{2,1,0:T(8,128)(2,1)S(1)}, u32[]{:S(2)}, u32[]{:S(2)}) async-start(bf16[32,248,128]{2,1,0:T(8,128)(2,1)} %front.1), calls=%async_computation | async-start | bytes 4063232 | tf_op jit(solution)/shard_map/all_to_all | solution.py:438
  14.3 0.0 copy-done
  14.3 25.7 %all_gather.6.refs_1_ = bf16[16,152,128]{2,1,0:T(8,128)(2,1)S(1)} all-gather(bf16[1,152,128]{2,1,0:T(8,128)(2,1)S(1)} %pack.1), channel_id=1, replica_groups=mesh['group'=32,'member'=16] {'member'}, dimensions={0}, use_global_device_ids=true | all-gather | bytes 661504 | tf_op jit(solution)/shard_map/all_gather | solution.py:442
  39.9 21.4 %all-to-all-done.refs_0_ = bf16[32,248,128]{2,1,0:T(8,128)(2,1)S(1)} async-done(((bf16[32,248,128]{2,1,0:T(8,128)(2,1)}), bf16[32,248,128]{2,1,0:T(8,128)(2,1)S(1)}, u32[]{:S(2)}, u32[]{:S(2)}) %all-to-all-start) | async-done | bytes 2031648 | tf_op jit(solution)/shard_map/all_to_all | solution.py:438
  61.4 2.3 %sweep.2 = (f32[8,152,128]{2,1,0:T(8,128)S(1)}, bf16[416,1280]{1,0:T(8,128)(2,1)S(1)}, f32[4,56,128]{2,1,0:T(8,128)S(1)}, bf16[1280,768]{1,0:T(8,128)(2,1)S(1)}, f32[1,1280]{1,0:T(1,128)S(1)}) custom-call(s32[1]{0:T(128)} %bitcast.core, bf16[32,248,128]{2,1,0:T(8,128)(2,1)S(1)} %all-to-all-done.refs_0_, bf16[16,152,128]{2,1,0:T(8,128)(2,1)S(1)} %all_gather.6.refs_1_), custom_call_target="tpu_custom_call" | custom-call | tf_op jit(solution)/shard_map/sweep/pallas_call | solution.py:335
  63.7 4.5 %collective-permute-start = (f32[8,152,128]{2,1,0:T(8,128)S(1)}, f32[8,152,128]{2,1,0:T(8,128)S(1)}, u32[]{:S(2)}, u32[]{:S(2)}) collective-permute-start(f32[8,152,128]{2,1,0:T(8,128)S(1)} %get-tuple-element.19), channel_id=1, source_target_pairs={{0,1},{1,0},{2,3},{3,2},{4,5},{5,4},{6,7},{7,6},{8,9},{9,8},{10,11... | collective-permute-start | bytes 1867784 | tf_op jit(solution)/shard_map/ppermute | solution.py:445
  68.2 0.8 kept.2.keep
  69.1 0.8 collective-permute-done.received
  69.9 0.1 join.2
  70.0 22.3 %all_to_all.15.parts = bf16[8,152,128]{2,1,0:T(8,128)(2,1)S(1)} all-to-all(bf16[8,152,128]{2,1,0:T(8,128)(2,1)S(1)} %join.2), channel_id=1, replica_groups={{0,2,4,6,8,10,12,14},{1,3,5,7,9,11,13,15},{16,18,20,22,24,26,28,30},{17..., dimensions={0} | all-to-all | bytes 622592 | tf_op jit(solution)/shard_map/all_to_all | solution.py:447
  92.2 0.1 update.2
  92.3 17.7 %all_gather.7.refs_2_ = bf16[16,152,128]{2,1,0:T(8,128)(2,1)S(1)} all-gather(bf16[1,152,128]{2,1,0:T(8,128)(2,1)S(1)} %get-tuple-element.20), channel_id=1, replica_groups=mesh['group'=32,'member'=16] {'member'}, dimensions={0}, use_global_device_ids=true | all-gather | bytes 661504 | tf_op jit(solution)/shard_map/all_gather | solution.py:442
  110.0 2.0 %sweep.3 = (f32[8,152,128]{2,1,0:T(8,128)S(1)}, bf16[416,1280]{1,0:T(8,128)(2,1)S(1)}, f32[4,56,128]{2,1,0:T(8,128)S(1)}) custom-call(s32[1]{0:T(128)} %bitcast.core, bf16[1280,768]{1,0:T(8,128)(2,1)S(1)} %get-tuple-element.15.items.refs_0_, f32[1,1280]{1,0:T(1,128)S(1)} %get-tuple-element.16.refs_1_, bf16[16,152,128]{2,1,0:T(8,128)(2,1)S(1)} %all_gather.7.refs_2_), custom_call_target="tpu_custom_call" | custom-call | tf_op jit(solution)/shard_map/sweep/pallas_call | solution.py:335
  112.0 2.1 %collective-permute-start.1 = (f32[8,152,128]{2,1,0:T(8,128)S(1)}, f32[8,152,128]{2,1,0:T(8,128)S(1)}, u32[]{:S(2)}, u32[]{:S(2)}) collective-permute-start(f32[8,152,128]{2,1,0:T(8,128)S(1)} %get-tuple-element.23), channel_id=1, source_target_pairs={{0,1},{1,0},{2,3},{3,2},{4,5},{5,4},{6,7},{7,6},{8,9},{9,8},{10,11... | collective-permute-start | bytes 1867784 | tf_op jit(solution)/shard_map/ppermute | solution.py:445
  114.1 0.8 kept.3.keep
  114.9 1.0 collective-permute-done.1.received
  115.9 0.1 join.3
  116.0 16.2 %all_to_all.16.parts = bf16[8,152,128]{2,1,0:T(8,128)(2,1)S(1)} all-to-all(bf16[8,152,128]{2,1,0:T(8,128)(2,1)S(1)} %join.3), channel_id=1, replica_groups={{0,2,4,6,8,10,12,14},{1,3,5,7,9,11,13,15},{16,18,20,22,24,26,28,30},{17..., dimensions={0} | all-to-all | bytes 622592 | tf_op jit(solution)/shard_map/all_to_all | solution.py:447
  132.1 0.7 update.3
  (1 shorter events, 0.0 us)
Async XLA Ops:
  3.6 10.7 %copy-start = (bf16[25,768]{1,0:T(8,128)(2,1)S(1)}, bf16[25,768]{1,0:T(8,128)(2,1)}, u32[]{:S(2)}) copy-start(bf16[25,768]{1,0:T(8,128)(2,1)} %prior.1) | copy-start | bytes 115204
  3.6 57.8 %all-to-all-start = ((bf16[32,248,128]{2,1,0:T(8,128)(2,1)}), bf16[32,248,128]{2,1,0:T(8,128)(2,1)S(1)}, u32[]{:S(2)}, u32[]{:S(2)}) async-start(bf16[32,248,128]{2,1,0:T(8,128)(2,1)} %front.1), calls=%async_computation | async-start | bytes 4063232 | tf_op jit(solution)/shard_map/all_to_all | solution.py:438
  63.7 6.2 %collective-permute-start = (f32[8,152,128]{2,1,0:T(8,128)S(1)}, f32[8,152,128]{2,1,0:T(8,128)S(1)}, u32[]{:S(2)}, u32[]{:S(2)}) collective-permute-start(f32[8,152,128]{2,1,0:T(8,128)S(1)} %get-tuple-element.19), channel_id=1, source_target_pairs={{0,1},{1,0},{2,3},{3,2},{4,5},{5,4},{6,7},{7,6},{8,9},{9,8},{10,11... | collective-permute-start | bytes 1867784 | tf_op jit(solution)/shard_map/ppermute | solution.py:445
  112.0 3.9 %collective-permute-start.1 = (f32[8,152,128]{2,1,0:T(8,128)S(1)}, f32[8,152,128]{2,1,0:T(8,128)S(1)}, u32[]{:S(2)}, u32[]{:S(2)}) collective-permute-start(f32[8,152,128]{2,1,0:T(8,128)S(1)} %get-tuple-element.23), channel_id=1, source_target_pairs={{0,1},{1,0},{2,3},{3,2},{4,5},{5,4},{6,7},{7,6},{8,9},{9,8},{10,11... | collective-permute-start | bytes 1867784 | tf_op jit(solution)/shard_map/ppermute | solution.py:445
